TPU v7x, 128 devices: a whole 4x4x4 slice. The times are simulated.
128 devices in a mesh: wide: 32 (over z_lo, y, x), dp: 4 (over z_hi, core).
Axes of the slice: x: 4, y: 4, z: 4 (z_hi: 2, z_lo: 2; z = z_hi * 2 + z_lo), core: 2. Of those that a mesh axis runs over, the one named last changes fastest.
Arguments:
- layer_input: bfloat16 [4, 8192, 4096], P('dp', 'wide'), may hold values from -6 to 6
- inner_acts: bfloat16 [4, 8192, 4096], P('dp', 'wide'), may hold values from -6 to 6
- w_bc: bfloat16 [4096, 256], replicated, may hold values from -0.0234375 to 0.0234375
- w_dt: bfloat16 [4096, 64], replicated, may hold values from -0.09375 to 0.09375
- a_log: float32 [64], replicated, may hold values from -20 to 2
- dt_bias: float32 [64], replicated, may hold values from -5 to -2
- d_skip: float32 [64], replicated, may hold values from 0.5 to 1.5
- out_grad: bfloat16 [4, 8192, 4096], P('dp', 'wide'), may hold values from -16 to 16
Outputs:
- x_grad: bfloat16 [4, 8192, 4096], P('dp', 'wide')
- input_grad: bfloat16 [4, 8192, 4096], P('dp', 'wide')
- w_bc_grad: float32 [4096, 256], P(('wide', 'dp'))
- w_dt_grad: float32 [4096, 64], P(('wide', 'dp'))
- head_grads: float32 [3, 64], P(None, 'wide')
All inputs are finite; a program needn't handle non-finite values.
Results may differ from a plain program's by a relative error of at most 0.03.
Values may be sent and summed in bfloat16 or wider, within the bound.
A program may use at most 448 MiB of HBM per device.

v0:
```python
import jax
import jax.numpy as jnp
from jax import lax
from jax.sharding import PartitionSpec as P

STRETCH = 256


precise = lax.Precision.HIGHEST


def stretch_forward(carried, pieces, a_log, d_skip):
    values, b_rows, c_rows, dt_pre = pieces
    steps_dt = jax.nn.softplus(dt_pre)
    log_rate = steps_dt * (-jnp.exp(a_log))[None, :]
    cumul = jnp.cumsum(log_rate, axis=0)
    length = values.shape[0]
    causal = jnp.arange(length)[:, None] >= jnp.arange(length)[None, :]
    gaps = cumul.T[:, :, None] - cumul.T[:, None, :]
    decay = jnp.exp(jnp.where(causal[None, :, :], gaps, -1e30))
    scores = jnp.dot(c_rows, b_rows.T, precision=precise)
    mixing = decay * scores[None, :, :] * steps_dt.T[:, None, :]
    within = jnp.einsum("hts,shp->thp", mixing, values, precision=precise)
    from_state = (
        jnp.einsum("tn,hpn->thp", c_rows, carried, precision=precise) * jnp.exp(cumul)[:, :, None]
    )
    output = within + from_state + d_skip[None, :, None] * values
    tail_weight = jnp.exp(cumul[-1][None, :] - cumul) * steps_dt
    fresh = jnp.einsum("sh,shp,sn->hpn", tail_weight, values, b_rows, precision=precise)
    updated = jnp.exp(cumul[-1])[:, None, None] * carried + fresh
    return (updated, output)


def run_sequence(values, b_rows, c_rows, dt_pre, a_log, d_skip, initial):
    blocks = values.shape[0] // STRETCH

    def split_blocks(array):
        return array.reshape((blocks, STRETCH) + array.shape[1:])

    def advance(carried, pieces):
        return stretch_forward(carried, pieces, a_log, d_skip)

    final, outputs = lax.scan(
        jax.checkpoint(advance),
        initial,
        (split_blocks(values), split_blocks(b_rows), split_blocks(c_rows), split_blocks(dt_pre)),
    )
    return (final, outputs.reshape(values.shape))


def local(layer_input, inner_acts, w_bc, w_dt, a_log, dt_bias, d_skip, out_grad):
    heads = a_log.shape[0]
    head_dim = inner_acts.shape[2] // heads
    state_width = w_bc.shape[1] // 2
    wide_count = lax.axis_size("wide")
    local_heads = heads // wide_count
    tok_rows = layer_input[0]
    bc_rows = jnp.dot(tok_rows, w_bc, preferred_element_type=jnp.float32).astype(jnp.bfloat16)
    dt_raw = jnp.dot(tok_rows, w_dt, preferred_element_type=jnp.float32).astype(jnp.bfloat16)
    head_inner, head_grad, head_dt = (
        lax.all_to_all(inner_acts, "wide", split_axis=2, concat_axis=1, tiled=True),
        lax.all_to_all(out_grad, "wide", split_axis=2, concat_axis=1, tiled=True),
        lax.all_to_all(dt_raw[None], "wide", split_axis=2, concat_axis=1, tiled=True),
    )
    all_bc = lax.all_gather(bc_rows[None], "wide", axis=1, tiled=True)[0]
    first_head = lax.axis_index("wide") * local_heads
    alog_local = lax.dynamic_slice_in_dim(a_log, first_head, local_heads)
    bias_local = lax.dynamic_slice_in_dim(dt_bias, first_head, local_heads)
    skip_local = lax.dynamic_slice_in_dim(d_skip, first_head, local_heads)
    length = head_inner.shape[1]
    values = head_inner[0].astype(jnp.float32).reshape(length, local_heads, head_dim)
    upstream = head_grad[0].astype(jnp.float32).reshape(length, local_heads, head_dim)
    b_rows = all_bc[:, :state_width].astype(jnp.float32)
    c_rows = all_bc[:, state_width:].astype(jnp.float32)
    dt_pre = head_dt[0].astype(jnp.float32) + bias_local[None, :]

    def forward(values_in, b_in, c_in, dt_in, alog_in, skip_in):
        initial = jnp.zeros((local_heads, head_dim, state_width), jnp.float32)
        return run_sequence(values_in, b_in, c_in, dt_in, alog_in, skip_in, initial)[1]

    _, pull = jax.vjp(forward, values, b_rows, c_rows, dt_pre, alog_local, skip_local)
    g_values, g_b, g_c, g_dt, g_alog, g_skip = pull(upstream)
    back_values, back_dt = (
        lax.all_to_all(
            g_values.reshape(length, local_heads * head_dim).astype(jnp.bfloat16)[None],
            "wide",
            split_axis=1,
            concat_axis=2,
            tiled=True,
        ),
        lax.all_to_all(
            g_dt.astype(jnp.bfloat16)[None], "wide", split_axis=1, concat_axis=2, tiled=True
        ),
    )
    g_dtraw = back_dt[0]
    d_bc = (
        lax.psum_scatter(
            jnp.concatenate([g_b, g_c], axis=1)[None].astype(jnp.bfloat16),
            "wide",
            scatter_dimension=1,
            tiled=True,
        )
        .astype(jnp.float32)[0]
        .astype(jnp.bfloat16)
    )
    head_grads = lax.psum(jnp.stack([g_alog, jnp.sum(g_dt, axis=0), g_skip]), "dp")
    d_input = (
        jnp.dot(d_bc, w_bc.T, preferred_element_type=jnp.float32)
        + jnp.dot(g_dtraw, w_dt.T, preferred_element_type=jnp.float32)
    ).astype(jnp.bfloat16)[None]
    proj_grad = jnp.concatenate([d_bc, g_dtraw], axis=1)
    weights_grad = lax.psum_scatter(
        lax.dot_general(
            tok_rows, proj_grad, (((0,), (0,)), ((), ())), preferred_element_type=jnp.float32
        ),
        ("wide", "dp"),
        scatter_dimension=0,
        tiled=True,
    )
    return (
        back_values,
        d_input,
        weights_grad[:, : 2 * state_width],
        weights_grad[:, 2 * state_width :],
        head_grads,
    )


def solution(mesh):
    in_specs = (
        P("dp", "wide", None),
        P("dp", "wide", None),
        P(),
        P(),
        P(),
        P(),
        P(),
        P("dp", "wide", None),
    )
    out_specs = (
        P("dp", "wide", None),
        P("dp", "wide", None),
        P(("wide", "dp"), None),
        P(("wide", "dp"), None),
        P(None, "wide"),
    )
    return jax.shard_map(local, mesh=mesh, in_specs=in_specs, out_specs=out_specs, check_vma=False)
```

profile of v0, /device:TPU:1, one launch (start us, length us, event | category | flops | bytes accessed | tf_op | source)
XLA Modules:
  0.0 2037.6 jit_solution(13904711306052207733)
XLA Ops:
  14.6 9.2 all-to-all-start
  23.8 10.0 copy.135
  33.8 22.9 %reduce.14 = bf16[4096,256]{1,0:T(8,128)(2,1)} reduce(bf16[4096,1,256]{2,1,0:T(2,128)(2,1)} %bitcast.405, bf16[]{:T(256)} %broadcast.118), dimensions={1}, to_apply=%bitcast.246.reduce_sub_computation | reduce | bytes 4194306
  60.7 7.9 all-to-all-start.1
  68.6 10.0 copy.136
  78.6 22.9 %reduce.15 = bf16[4096,256]{1,0:T(8,128)(2,1)} reduce(bf16[4096,1,256]{2,1,0:T(2,128)(2,1)} %bitcast.406, bf16[]{:T(256)} %broadcast.118), dimensions={1}, to_apply=%bitcast.248.reduce_sub_computation | reduce | bytes 4194306
  105.5 8.0 all-to-all-start.2
  115.9 10.5 reshape.328
  126.3 6.5 convert_bitcast_fusion.1
  135.2 11.4 all-to-all-done.2
  146.6 10.5 reshape.330
  157.1 6.5 convert_bitcast_fusion
  166.1 4.6 all-gather.3.cloned.1.call-done
  178.0 148.7 %while.40 = (s32[]{:T(128)}, f32[2,64,128]{2,1,0:T(8,128)S(1)}, f32[32,2,64,128]{3,2,1,0:T(8,128)}, f32[32,256,2]{1,2,0:T(2,128)}, f32[1,2]{1,0:T(1,128)S(1)}, /...) while((s32[]{:T(128)}, f32[2,64,128]{2,1,0:T(8,128)S(1)}, ...), condition=%wide.region_3.4_spmd.clone, body=%wide.region_0.3_spmd.clone.sunk | while | flops 50503176 | bytes 554779 | solution.py:43
  332.5 850.1 %while.41 = (s32[]{:T(128)}, f32[2]{0:T(128)}, f32[2]{0:T(128)}, f32[2,64,128]{2,1,0:T(8,128)}, bf16[32,256,2,64]{1,3,2,0:T(8,128)(2,1)}, /*index=5*/bf16[32,256...) while((s32[]{:T(128)}, f32[2]{0:T(128)}, f32[2]{0:T(128)}, ...), condition=%wide.region_18.19_spmd.clone, body=%wide.region_4.18_spmd.clone.sunk | while | flops 757923328 | bytes 7403913 | solution.py:43
  1182.6 4.6 pad_maximum_fusion
  1188.2 7.2 copy.140
  1195.4 46.5 %reduce.17 = bf16[8192,2]{1,0:T(8,128)(2,1)} reduce(bf16[8192,1,2]{2,1,0:T(2,128)(2,1)} %bitcast.410, bf16[]{:T(256)} %broadcast.118), dimensions={1}, to_apply=%bitcast.252.reduce_sub_computation | reduce | bytes 65538
  1241.9 4.2 reshape.333
  1246.1 13.1 all_to_all.60
  1259.2 8.4 reshape.334
  1267.6 8.1 copy.141
  1275.9 76.0 %reduce-scatter.5.cloned.1.call-done = bf16[1,256,256]{2,1,0:T(8,128)(2,1)} async-done(((bf16[1,8192,256]{2,1,0:T(8,128)(2,1)}), bf16[1,256,256]{2,1,0:T(8,128)(2,1)}) %reduce-scatter.5.cloned.1.call-update) | async-done | bytes 131088 | tf_op jit(solution)/shard_map/reduce_scatter | solution.py:97
  1351.9 4.2 convolution_bitcast_fusion.3
  1356.0 6.3 copy.153
  1362.4 10.0 copy.152
  1372.4 16.2 reshape.317
  1388.6 46.5 %reduce.16 = bf16[8192,128]{1,0:T(8,128)(2,1)} reduce(bf16[8192,1,128]{2,1,0:T(2,128)(2,1)} %bitcast.407, bf16[]{:T(256)} %broadcast.118), dimensions={1}, to_apply=%bitcast.250.reduce_sub_computation | reduce | bytes 4194306
  1439.0 4.9 all-to-all-start.3
  1444.6 29.6 %psum.7 = f32[3,2]{1,0:T(4,128)S(1)} all-reduce(f32[3,2]{1,0:T(4,128)S(1)} %pad_maximum_fusion.1), channel_id=1, replica_groups=mesh['wide'=32,'dp'=4] {'dp'}, use_global_device_ids=true, to_apply=%region_22.23 | all-reduce | flops 6 | bytes 48 | tf_op jit(solution)/shard_map/psum | solution.py:106
  1474.9 10.5 reshape.332
  1501.8 526.4 %reduce-scatter.7.cloned.1.call-done = f32[32,320]{1,0:T(8,128)} async-done(((f32[4096,320]{1,0:T(8,128)}), f32[32,320]{1,0:T(8,128)}) %reduce-scatter.7.cloned.1.call-update) | async-done | bytes 40976
  (2086 shorter events, 1056.3 us)
Async XLA Ops:
  7.2 163.4 %all-gather.3.cloned.1.call-start = ((), (), s32[]{:S(2)}) async-start(), calls=%async_computation.8 | async-start | bytes 4325376 | tf_op jit(solution)/shard_map/all_gather | solution.py:65
  14.6 46.1 %all-to-all-start = ((bf16[32,2,256]{2,1,0:T(2,128)(2,1)}), bf16[32,2,256]{2,1,0:T(2,128)(2,1)S(1)}, u32[]{:S(2)}, u32[]{:S(2)}) async-start(bf16[32,2,256]{2,1,0:T(2,128)(2,1)} %reshape.325), calls=%async_computation | async-start | bytes 65536 | tf_op jit(solution)/shard_map/all_to_all | solution.py:63
  60.7 44.8 %all-to-all-start.1 = ((bf16[32,2,16384]{2,1,0:T(2,128)(2,1)}), bf16[32,2,16384]{2,1,0:T(2,128)(2,1)}, u32[]{:S(2)}, u32[]{:S(2)}) async-start(bf16[32,2,16384]{2,1,0:T(2,128)(2,1)} %reshape.327), calls=%async_computation.1 | async-start | bytes 4194304 | tf_op jit(solution)/shard_map/all_to_all | solution.py:61
  105.5 41.2 %all-to-all-start.2 = ((bf16[32,2,16384]{2,1,0:T(2,128)(2,1)}), bf16[32,2,16384]{2,1,0:T(2,128)(2,1)}, u32[]{:S(2)}, u32[]{:S(2)}) async-start(bf16[32,2,16384]{2,1,0:T(2,128)(2,1)} %reshape.329), calls=%async_computation.2 | async-start | bytes 4194304 | tf_op jit(solution)/shard_map/all_to_all | solution.py:62
  113.4 1238.4 %reduce-scatter.5.cloned.1.call-start = ((), (), s32[]{:S(2)}) async-start(), calls=%async_computation.7 | async-start | bytes 4325376 | tf_op jit(solution)/shard_map/reduce_scatter | solution.py:97
  358.3 10.4 copy-start.3
  438.1 10.4 copy-start.3
  464.7 10.4 copy-start.3
  491.4 10.4 copy-start.3
  517.9 10.4 copy-start.3
  544.6 10.4 copy-start.3
  624.4 10.4 copy-start.3
  677.6 10.4 copy-start.3
  704.3 10.4 copy-start.3
  730.8 10.4 copy-start.3
  757.4 10.4 copy-start.3
  784.1 10.4 copy-start.3
  810.7 10.4 copy-start.3
  837.3 10.4 copy-start.3
  863.9 10.4 copy-start.3
  890.5 10.4 copy-start.3
  917.2 10.4 copy-start.3
  943.8 10.4 copy-start.3
  970.4 10.4 copy-start.3
  997.0 10.4 copy-start.3
  1050.2 10.4 copy-start.3
  1076.9 10.4 copy-start.3
  1103.4 10.4 copy-start.3
  1130.1 10.4 copy-start.3
  1156.7 10.4 copy-start.3
  1187.2 841.0 %reduce-scatter.7.cloned.1.call-start = ((), (), s32[]{:S(2)}) async-start(), calls=%async_computation.9 | async-start | bytes 6340608
  1439.0 35.8 %all-to-all-start.3 = ((bf16[32,2,16384]{2,1,0:T(2,128)(2,1)}), bf16[32,2,16384]{2,1,0:T(2,128)(2,1)}, u32[]{:S(2)}, u32[]{:S(2)}) async-start(bf16[32,2,16384]{2,1,0:T(2,128)(2,1)} %reshape.331), calls=%async_computation.3 | async-start | bytes 4194304 | tf_op jit(solution)/shard_map/all_to_all | solution.py:84
  (144 other events, 611.7 us)
Sparse Core Ops, SparseCore 0:
  11.8 158.7 all-gather.2
  1187.3 164.4 reduce-scatter.4
  1362.5 665.6 reduce-scatter.6
where the time goes:
time: 2070 us; the launch traced here: 2040 us
  other arithmetic  627 us (30%)
  waiting for transfers between devices  618 us (30%)
  matrix products  364 us (18%)
  local copies, waits for them, and re-layouts  338 us (16%)
  blocking collectives  42.7 us (2%)
  starting transfers between devices  30.2 us (1%)
    unnamed x4, waiting for transfers between devices  526 us
    another operation x224, other arithmetic  157 us
    unnamed x9, other arithmetic  140 us
    dot_general x64, matrix products, stretch_forward(): within = jnp.einsum('hts,shp->thp', mixing, values, precision=precise)  113 us
    squeeze x128, local copies, waits for them, and re-layouts, run_sequence(): lax.scan(jax.checkpoint(advance), initial, (split_blocks(values), split_b...  112 us
    unnamed x38, local copies, waits for them, and re-layouts  99.2 us
    dot_general x96, matrix products, stretch_forward(): jnp.einsum('sh,shp,sn->hpn', tail_weight, values, b_rows, precision=precise)  83.6 us
    dot_general x96, matrix products, stretch_forward(): scores = jnp.dot(c_rows, b_rows.T, precision=precise)  83.3 us
  transfers between devices with their start and end apart: 7, of which 4 were waited for; matrix products, arithmetic and copies ran while one was open for 15% of the time, Pallas kernels for 0%

commit v1 on v0

v1 whole, which is shorter than its diff:
```python
import functools

import jax
import jax.numpy as jnp
from jax import lax
from jax.experimental import pallas as pl
from jax.experimental.pallas import tpu as pltpu
from jax.sharding import PartitionSpec as P

MESH = pl.DeviceIdType.MESH
BF = jnp.bfloat16
F32 = jnp.float32
LANES = 128
BLOCK = 512


def mm(a, b):
    return jnp.dot(a, b, preferred_element_type=F32)


def mm_nt(a, b):
    return lax.dot_general(a, b, (((1,), (1,)), ((), ())), preferred_element_type=F32)


def split2(v):
    hi = v.astype(BF)
    return hi, (v - hi.astype(F32)).astype(BF)


def split3(v):
    hi = v.astype(BF)
    rest = v - hi.astype(F32)
    mid = rest.astype(BF)
    return hi, mid, (rest - mid.astype(F32)).astype(BF)


def scan_kernel(
    wide, dp, in_hbm, x_hbm, g_hbm, wbc_hbm, wdt_hbm, alog_ref, bias_ref, skip_ref,
    xg_hbm, ig_hbm, wpart_ref,
    in_ref, x_ref, g_ref, wbc_ref, wdt_ref, fg_ref, got1_ref, back_ref, got2_ref,
    xs_ref, gs_ref, gxw_ref, int_ref, nt_ref, st_ref, lt_ref, rt_ref, col_ref, hrow_ref, srow_ref,
    xo_ref, io_ref, load_sem, store_sem, s1_sem, r1_sem, s2_sem, r2_sem,
):
    me = lax.axis_index("wide")
    seq, width = in_ref.shape
    heads = alog_ref.shape[1]
    half = seq // 2
    nst = wbc_ref.shape[1] // 2
    owners = BLOCK // LANES
    blocks = width // BLOCK
    per_block = BLOCK // 64

    barrier = pltpu.get_barrier_semaphore()

    def greet(k, _):
        pl.semaphore_signal(
            barrier, inc=1, device_id={"wide": lax.rem(me + k, wide)}, device_id_type=MESH
        )
        return 0

    lax.fori_loop(1, wide, greet, 0)

    loads = [
        pltpu.make_async_copy(src, dst, load_sem.at[i])
        for i, (src, dst) in enumerate(
            ((in_hbm, in_ref), (wbc_hbm, wbc_ref), (wdt_hbm, wdt_ref), (x_hbm, x_ref), (g_hbm, g_ref))
        )
    ]
    for load in loads:
        load.start()
    loads[0].wait()
    loads[1].wait()
    bc = mm(in_ref[...], wbc_ref[...]).astype(BF)
    loads[2].wait()
    dt_raw = mm(in_ref[...], wdt_ref[...]).astype(BF).astype(F32)
    b_rows = bc[:, :nst]
    c_rows = bc[:, nst:]
    b_t = b_rows.astype(F32).T.astype(BF)
    c_t = c_rows.astype(F32).T.astype(BF)
    dt_pre = dt_raw + bias_ref[...]
    dt = jnp.maximum(dt_pre, 0.0) + jnp.log1p(jnp.exp(-jnp.abs(dt_pre)))
    rate = -jnp.exp(alog_ref[...])
    log_rate = dt * rate
    pos_r = lax.broadcasted_iota(jnp.int32, (seq, seq), 0)
    pos_c = lax.broadcasted_iota(jnp.int32, (seq, seq), 1)
    lower = (pos_r >= pos_c).astype(BF)
    lr_hi, lr_mid, lr_lo = split3(log_rate)
    cumul = mm(lower, lr_hi) + mm(lower, lr_mid) + mm(lower, lr_lo)
    last = cumul[seq - 1 :, :]
    tail = dt * jnp.exp(last - cumul)
    head_exp = jnp.exp(cumul)
    tail2 = jnp.concatenate(split2(tail), axis=1)
    exp2 = jnp.concatenate(split2(head_exp), axis=1)
    lq_hi, lq_mid, lq_lo = split3(last)
    none = jnp.zeros((1, heads), BF)
    lq_rows = jnp.concatenate(
        [jnp.concatenate([v, none], axis=1) for v in (lq_hi, lq_mid, lq_lo)]
        + [jnp.zeros((13, 2 * heads), BF)],
        axis=0,
    )
    lt_ref[...] = cumul.T
    u3 = jnp.concatenate(split3(jnp.log(jnp.maximum(dt, 1e-37)) - cumul), axis=1)
    st_ref[...] = mm_nt(b_rows, c_rows)

    delta = lax.rem(
        lax.broadcasted_iota(jnp.int32, (2 * heads, BLOCK), 0), heads
    ) - lax.broadcasted_iota(jnp.int32, (2 * heads, BLOCK), 1) // 64

    def spread(j):
        return (delta == j * per_block).astype(BF)

    loads[3].wait()
    loads[4].wait()
    pl.semaphore_wait(barrier, wide - 1)

    def first_copy(peer):
        return pltpu.make_async_remote_copy(
            src_ref=fg_ref.at[peer],
            dst_ref=got1_ref.at[me],
            send_sem=s1_sem.at[peer],
            recv_sem=r1_sem.at[me],
            device_id={"wide": peer},
            device_id_type=MESH,
        )

    def second_copy(peer):
        return pltpu.make_async_remote_copy(
            src_ref=back_ref.at[peer],
            dst_ref=got2_ref.at[me],
            send_sem=s2_sem.at[peer],
            recv_sem=r2_sem.at[me],
            device_id={"wide": peer},
            device_id_type=MESH,
        )

    def fresh(step, _):
        j = lax.rem(step + me // owners + 1, blocks)
        cols = pl.ds(pl.multiple_of(j * BLOCK, BLOCK), BLOCK)
        r = spread(j)
        xs = (x_ref[:, cols].astype(F32) * mm(tail2, r)).astype(BF)
        xs_ref[:, cols] = xs
        f_t = mm(b_t, xs).astype(BF)
        gs = (g_ref[:, cols].astype(F32) * mm(exp2, r)).astype(BF)
        gs_ref[:, cols] = gs
        g_t = mm(c_t, gs).astype(BF)
        lq = mm(lq_rows, r).astype(BF)
        for i in range(owners):
            lanes = slice(i * LANES, (i + 1) * LANES)
            peer = j * owners + i
            fg_ref[peer, :nst, :] = f_t[:, lanes]
            fg_ref[peer, nst : 2 * nst, :] = g_t[:, lanes]
            fg_ref[peer, 2 * nst :, :] = lq[:, lanes]

            @pl.when(peer != me)
            def _():
                first_copy(peer).start()

        return 0

    lax.fori_loop(0, blocks, fresh, 0)

    lane = lax.broadcasted_iota(jnp.int32, (seq, LANES), 1)
    lane_head = lax.broadcasted_iota(jnp.int32, (half, heads), 1)
    upper = lax.broadcasted_iota(jnp.int32, (half, half), 0) <= lax.broadcasted_iota(
        jnp.int32, (half, half), 1
    )
    row_head = lax.rem(lax.broadcasted_iota(jnp.int32, (3 * heads, LANES), 0), heads)
    nt_ref[...] = jnp.zeros_like(nt_ref)
    col_ref[...] = jnp.zeros_like(col_ref)

    def within(pair, _):
        cols = pl.ds(pl.multiple_of(pair * LANES, LANES), LANES)
        xk = x_ref[:, cols]
        gk = g_ref[:, cols]
        total_lo = jnp.zeros((half, LANES), F32)
        total_hi = jnp.zeros((half, LANES), F32)
        for side in range(2):
            h = pair * 2 + side
            mine = (lane < 64) if side == 0 else (lane >= 64)
            xm = jnp.where(mine, xk, jnp.zeros_like(xk))
            gm = jnp.where(mine, gk, jnp.zeros_like(gk))
            u = mm(u3, (row_head == h).astype(BF))
            lt = lt_ref[pl.ds(h, 1), :]
            w0 = mm_nt(xm[:half], gk)
            w1 = mm_nt(xm[half:], gk[half:])
            a00 = jnp.where(upper, jnp.exp(u[:half] + lt[:, :half]), 0.0)
            a01 = jnp.exp(u[:half] + lt[:, half:])
            a11 = jnp.where(upper, jnp.exp(u[half:] + lt[:, half:]), 0.0)
            s00 = st_ref[:half, :half]
            s01 = st_ref[:half, half:]
            s11 = st_ref[half:, half:]
            p00 = a00 * w0[:, :half]
            p01 = a01 * w0[:, half:]
            p11 = a11 * w1
            nt_ref[:half, :half] += p00
            nt_ref[:half, half:] += p01
            nt_ref[half:, half:] += p11
            total_lo += mm((a00 * s00).astype(BF), gm[:half]) + mm((a01 * s01).astype(BF), gm[half:])
            total_hi += mm((a11 * s11).astype(BF), gm[half:])
            z00 = p00 * s00
            z01 = p01 * s01
            z11 = p11 * s11
            rt_ref[h, :, :half] = jnp.sum(z00, axis=0, keepdims=True)
            rt_ref[h, :, half:] = jnp.sum(z01 + z11, axis=0, keepdims=True)
            col_ref[:half, :] += jnp.where(
                lane_head == h, jnp.sum(z00 + z01, axis=1, keepdims=True), 0.0
            )
            col_ref[half:, :] += jnp.where(
                lane_head == h, jnp.sum(z11, axis=1, keepdims=True), 0.0
            )
        gxw_ref[:half, cols] = total_lo
        gxw_ref[half:, cols] = total_hi
        int_ref[cols, :] = in_ref[:, cols].astype(F32).T.astype(BF)
        return 0

    pairs = width // LANES
    lax.fori_loop(0, pairs // 2, within, 0)

    got1_ref[me] = fg_ref[me]

    def take1(k, _):
        peer = lax.rem(me + k, wide)
        pltpu.make_async_copy(fg_ref.at[peer], got1_ref.at[peer], r1_sem.at[peer]).wait()
        return 0

    lax.fori_loop(1, wide, take1, 0)

    def decay_of(i):
        parts = got1_ref[i, 2 * nst :, :].astype(F32)
        return jnp.exp(parts[0:1] + parts[1:2] + parts[2:3])

    def advance(i, carried):
        state, pull = carried
        later = wide - 1 - i
        back_ref[i, :nst, :] = state.astype(BF)
        back_ref[later, nst:, :] = pull.astype(BF)
        state = state * decay_of(i) + got1_ref[i, :nst, :].astype(F32)
        pull = pull * decay_of(later) + got1_ref[later, nst : 2 * nst, :].astype(F32)
        return state, pull

    start = jnp.zeros((nst, LANES), F32)
    lax.fori_loop(0, wide, advance, (start, start))

    def give2(k, _):
        second_copy(lax.rem(me + k, wide)).start()
        return 0

    lax.fori_loop(1, wide, give2, 0)
    got2_ref[me] = back_ref[me]

    lax.fori_loop(pairs // 2, pairs, within, 0)

    n_low = nt_ref[...].astype(BF)
    g_b = mm(n_low, c_rows)
    g_c = mm(nt_ref[...].T.astype(BF), b_rows)

    def take2(k, _):
        peer = lax.rem(me + k, wide)
        pltpu.make_async_copy(back_ref.at[peer], got2_ref.at[peer], r2_sem.at[peer]).wait()
        first_copy(peer).wait_send()
        second_copy(peer).wait_send()
        return 0

    lax.fori_loop(1, wide, take2, 0)

    skip_hi, skip_lo = split2(skip_ref[...])
    skip_rows = jnp.concatenate(
        [jnp.concatenate([skip_hi, skip_lo], axis=1)]
        + [jnp.concatenate([v, none], axis=1) for v in (lq_hi, lq_mid, lq_lo)]
        + [jnp.zeros((12, 2 * heads), BF)],
        axis=0,
    )
    gather_delta = lax.broadcasted_iota(jnp.int32, (BLOCK, heads), 1) - lax.broadcasted_iota(
        jnp.int32, (BLOCK, heads), 0
    ) // 64

    def finish(j, carried):
        row_st, col_st, gb, gc = carried
        cols = pl.ds(pl.multiple_of(j * BLOCK, BLOCK), BLOCK)
        r = spread(j)
        gather = (gather_delta == j * per_block).astype(BF)
        h0 = jnp.concatenate([got2_ref[j * owners + i, :nst, :] for i in range(owners)], axis=1)
        dh = jnp.concatenate([got2_ref[j * owners + i, nst:, :] for i in range(owners)], axis=1)
        own = jnp.concatenate([fg_ref[j * owners + i, :nst, :] for i in range(owners)], axis=1)
        xs = xs_ref[:, cols]
        gs = gs_ref[:, cols]
        g32 = g_ref[:, cols].astype(F32)
        y_st = mm(c_rows, h0)
        u_st = mm(b_rows, dh)
        rows = mm(skip_rows, r)
        gx = gxw_ref[:, cols] + mm(tail2, r) * u_st + rows[0:1] * g32
        xo_ref[:, cols] = gx.astype(BF)
        row_st += mm((gs.astype(F32) * y_st).astype(BF), gather)
        col_st += mm((xs.astype(F32) * u_st).astype(BF), gather)
        gb += mm_nt(xs, dh)
        gc += mm_nt(gs, h0)
        ended = h0.astype(F32) * jnp.exp(rows[1:2] + rows[2:3] + rows[3:4]) + own.astype(F32)
        hrow_ref[0:1, cols] = jnp.sum(ended * dh.astype(F32), axis=0, keepdims=True)
        hrow_ref[1:2, cols] = jnp.sum(x_ref[:, cols].astype(F32) * g32, axis=0, keepdims=True)
        pltpu.make_async_copy(xo_ref.at[:, cols], xg_hbm.at[:, cols], store_sem.at[0, j]).start()
        return row_st, col_st, gb, gc

    zero_h = jnp.zeros((seq, heads), F32)
    row_st, col_st, g_b, g_c = lax.fori_loop(0, blocks, finish, (zero_h, zero_h, g_b, g_c))

    head_of = lax.broadcasted_iota(jnp.int32, (width, heads), 0) // 64
    gather_all = (head_of == lax.broadcasted_iota(jnp.int32, (width, heads), 1)).astype(BF)
    hr_hi, hr_lo = split2(hrow_ref[...])
    sums = mm(hr_hi, gather_all) + mm(hr_lo, gather_all)
    crossing, g_skip = sums[0:1], sums[1:2]

    row_all = rt_ref[:, 0, :].T + row_st
    col_all = col_ref[...] + col_st
    upper_all = (pos_r <= pos_c).astype(BF)
    d_hi, d_mid, d_lo = split3(row_all - col_all)
    d_log = mm(upper_all, d_hi) + mm(upper_all, d_mid) + mm(upper_all, d_lo) + crossing
    gate = 1.0 / (1.0 + jnp.exp(-dt_pre))
    ratio = jnp.where(dt > 0.0, gate / jnp.where(dt > 0.0, dt, 1.0), 1.0)
    g_dt = col_all * ratio + rate * d_log * gate
    g_alog = jnp.sum(d_log * log_rate, axis=0, keepdims=True)
    g_bias = jnp.sum(g_dt, axis=0, keepdims=True)
    d_bc = jnp.concatenate([g_b, g_c], axis=1).astype(BF)
    g_raw = g_dt.astype(BF)
    head_rows = jnp.concatenate([g_alog, g_bias, g_skip, jnp.zeros((13, heads), F32)], axis=0)
    head_rows = jnp.concatenate(split2(head_rows), axis=1)

    def emit(j, _):
        cols = pl.ds(pl.multiple_of(j * BLOCK, BLOCK), BLOCK)
        d_in = mm_nt(d_bc, wbc_ref[cols, :]) + mm_nt(g_raw, wdt_ref[cols, :])
        io_ref[:, cols] = d_in.astype(BF)
        pltpu.make_async_copy(io_ref.at[:, cols], ig_hbm.at[:, cols], store_sem.at[1, j]).start()
        rows = int_ref[cols, :]
        w_bc = mm(rows, d_bc).astype(BF)
        w_dt = mm(rows, g_raw)
        for i in range(BLOCK // 32):
            d = i % dp
            slot = (j * (BLOCK // 32 // dp) + i // dp) * (dp // 2) + d // 2
            at = slice(i * 32, (i + 1) * 32)
            wpart_ref[d % 2, slot, 0:32, :] = w_bc[at, :LANES]
            wpart_ref[d % 2, slot, 32:64, :] = w_bc[at, LANES:]
            wpart_ref[d % 2, slot, 64:80, : 2 * heads] = jnp.concatenate(
                [w_dt[i * 32 : i * 32 + 16], w_dt[i * 32 + 16 : i * 32 + 32]], axis=1
            ).astype(BF)
            wpart_ref[d % 2, slot, 80:96, : 2 * heads] = head_rows
        return 0

    lax.fori_loop(0, blocks, emit, 0)

    def drain(j, _):
        cols = pl.ds(pl.multiple_of(j * BLOCK, BLOCK), BLOCK)
        pltpu.make_async_copy(xo_ref.at[:, cols], xg_hbm.at[:, cols], store_sem.at[0, j]).wait()
        pltpu.make_async_copy(io_ref.at[:, cols], ig_hbm.at[:, cols], store_sem.at[1, j]).wait()
        return 0

    lax.fori_loop(0, blocks, drain, 0)


def sum_kernel(
    wide, dp, heads, wpart_ref, wbc_out, wdt_out, head_out,
    pair_ref, sent_ref, got_ref, sp_sem, rp_sem, s_sem, r_sem,
):
    me = lax.axis_index("wide")
    place = lax.axis_index("dp")
    core = lax.rem(place, 2)
    other = 1 - core
    sets = dp // 2
    mine = me * sets + place // 2
    slots = wide * sets
    group = 8
    groups = slots // group
    sibling = {"wide": me, "dp": place - core + other}

    def at_slot(slot):
        return {"wide": slot // sets, "dp": lax.rem(slot, sets) * 2 + core}

    barrier = pltpu.get_barrier_semaphore()
    pl.semaphore_signal(barrier, inc=1, device_id=sibling, device_id_type=MESH)

    def greet(k, _):
        pl.semaphore_signal(
            barrier, inc=1, device_id=at_slot(lax.rem(mine + k, slots)), device_id_type=MESH
        )
        return 0

    lax.fori_loop(1, slots, greet, 0)
    pl.semaphore_wait(barrier, slots)

    def pair_copy(c):
        part = pl.ds(c * group, group)
        return pltpu.make_async_remote_copy(
            src_ref=wpart_ref.at[other, part],
            dst_ref=pair_ref.at[part],
            send_sem=sp_sem.at[c],
            recv_sem=rp_sem.at[c],
            device_id=sibling,
            device_id_type=MESH,
        )

    def slot_copy(slot):
        return pltpu.make_async_remote_copy(
            src_ref=sent_ref.at[slot],
            dst_ref=got_ref.at[mine],
            send_sem=s_sem.at[slot],
            recv_sem=r_sem.at[mine],
            device_id=at_slot(slot),
            device_id_type=MESH,
        )

    def turn(k):
        return lax.rem(mine // group + k + 1, groups)

    def give(k, _):
        pair_copy(turn(k)).start()
        return 0

    lax.fori_loop(0, groups, give, 0)

    def add(k, _):
        c = turn(k)
        pair_copy(c).wait_recv()
        for i in range(group):
            slot = c * group + i
            sent_ref[slot, :80, :] = (
                wpart_ref[core, slot, :80, :].astype(F32) + pair_ref[slot, :80, :].astype(F32)
            ).astype(BF)
            ours = wpart_ref[core, slot, 80:, :].astype(F32)
            theirs = pair_ref[slot, 80:, :].astype(F32)
            both = ours + theirs
            sent_ref[slot, 80:, : 2 * heads] = jnp.concatenate(
                split2(both[:, :heads] + both[:, heads : 2 * heads]), axis=1
            )

            @pl.when(slot != mine)
            def _():
                slot_copy(slot).start()

        return 0

    lax.fori_loop(0, groups, add, 0)

    def total(k, acc):
        slot = lax.rem(mine + k, slots)
        pltpu.make_async_copy(sent_ref.at[slot], got_ref.at[slot], r_sem.at[slot]).wait()
        return acc + got_ref[slot].astype(F32)

    acc = lax.fori_loop(1, slots, total, sent_ref[mine].astype(F32))
    wbc_out[:, :LANES] = acc[0:32]
    wbc_out[:, LANES:] = acc[32:64]
    wdt_out[0:16, :] = acc[64:80, :heads]
    wdt_out[16:32, :] = acc[64:80, heads : 2 * heads]
    rows = acc[80:88, :heads] + acc[80:88, heads : 2 * heads]
    at = lax.broadcasted_iota(jnp.int32, rows.shape, 1)
    per = heads // wide
    for i in range(per):
        picked = jnp.sum(jnp.where(at == me * per + i, rows, 0.0), axis=1, keepdims=True)
        head_out[:, i : i + 1] = picked[:3]

    def done(k, _):
        slot_copy(lax.rem(mine + k, slots)).wait_send()
        return 0

    lax.fori_loop(1, slots, done, 0)

    def done_pair(c, _):
        pair_copy(c).wait_send()
        return 0

    lax.fori_loop(0, groups, done_pair, 0)


def local(wide, dp, layer_input, inner_acts, w_bc, w_dt, a_log, dt_bias, d_skip, out_grad):
    seq, width = layer_input.shape[1:]
    heads = a_log.shape[0]
    nst = w_bc.shape[1] // 2
    slots = wide * dp // 2
    any_spec = pl.BlockSpec(memory_space=pl.ANY)
    vmem = pl.BlockSpec(memory_space=pltpu.VMEM)
    dma = pltpu.SemaphoreType.DMA
    x_grad, input_grad, wpart = pl.pallas_call(
        functools.partial(scan_kernel, wide, dp),
        out_shape=(
            jax.ShapeDtypeStruct((seq, width), BF),
            jax.ShapeDtypeStruct((seq, width), BF),
            jax.ShapeDtypeStruct((2, slots, 96, LANES), BF),
        ),
        in_specs=[any_spec] * 5 + [vmem] * 3,
        out_specs=(any_spec, any_spec, vmem),
        scratch_shapes=[
            pltpu.VMEM((seq, width), BF),
            pltpu.VMEM((seq, width), BF),
            pltpu.VMEM((seq, width), BF),
            pltpu.VMEM((width, 2 * nst), BF),
            pltpu.VMEM((width, heads), BF),
            pltpu.VMEM((wide, 2 * nst + 16, LANES), BF),
            pltpu.VMEM((wide, 2 * nst + 16, LANES), BF),
            pltpu.VMEM((wide, 2 * nst, LANES), BF),
            pltpu.VMEM((wide, 2 * nst, LANES), BF),
            pltpu.VMEM((seq, width), BF),
            pltpu.VMEM((seq, width), BF),
            pltpu.VMEM((seq, width), F32),
            pltpu.VMEM((width, seq), BF),
            pltpu.VMEM((seq, seq), F32),
            pltpu.VMEM((seq, seq), F32),
            pltpu.VMEM((heads, seq), F32),
            pltpu.VMEM((heads, 1, seq), F32),
            pltpu.VMEM((seq, heads), F32),
            pltpu.VMEM((2, width), F32),
            pltpu.VMEM((2, width), F32),
            pltpu.VMEM((seq, width), BF),
            pltpu.VMEM((seq, width), BF),
            dma((5,)),
            dma((2, width // BLOCK)),
            dma((wide,)),
            dma((wide,)),
            dma((wide,)),
            dma((wide,)),
        ],
        compiler_params=pltpu.CompilerParams(
            collective_id=0, has_side_effects=True, vmem_limit_bytes=56 * 1024 * 1024
        ),
        cost_estimate=pl.CostEstimate(
            flops=30 * seq * width * 256, bytes_accessed=8 * seq * width, transcendentals=0
        ),
        name="scan_backward",
    )(
        layer_input[0], inner_acts[0], out_grad[0], w_bc, w_dt,
        a_log[None], dt_bias[None], d_skip[None],
    )
    rows = width // (wide * dp)
    wbc_grad, wdt_grad, head_grads = pl.pallas_call(
        functools.partial(sum_kernel, wide, dp, heads),
        out_shape=(
            jax.ShapeDtypeStruct((rows, 2 * nst), F32),
            jax.ShapeDtypeStruct((rows, heads), F32),
            jax.ShapeDtypeStruct((3, heads // wide), F32),
        ),
        in_specs=[vmem],
        out_specs=(vmem, vmem, vmem),
        scratch_shapes=[
            pltpu.VMEM((slots, 96, LANES), BF),
            pltpu.VMEM((slots, 96, LANES), BF),
            pltpu.VMEM((slots, 96, LANES), BF),
            dma((slots // 8,)),
            dma((slots // 8,)),
            dma((slots,)),
            dma((slots,)),
        ],
        compiler_params=pltpu.CompilerParams(
            collective_id=1, has_side_effects=True, vmem_limit_bytes=24 * 1024 * 1024
        ),
        name="weight_sums",
    )(wpart)
    return x_grad[None], input_grad[None], wbc_grad, wdt_grad, head_grads


def solution(mesh):
    in_specs = (
        P("dp", "wide", None),
        P("dp", "wide", None),
        P(),
        P(),
        P(),
        P(),
        P(),
        P("dp", "wide", None),
    )
    out_specs = (
        P("dp", "wide", None),
        P("dp", "wide", None),
        P(("wide", "dp"), None),
        P(("wide", "dp"), None),
        P(None, "wide"),
    )
    return jax.shard_map(
        functools.partial(local, mesh.shape["wide"], mesh.shape["dp"]),
        mesh=mesh,
        in_specs=in_specs,
        out_specs=out_specs,
        check_vma=False,
    )
```

time: 2070 us -> 133 us (0.06); the launches traced: 2040 us -> 133 us
  other arithmetic: 627 us -> 0 us
  waiting for transfers between devices: 618 us -> 0 us
  matrix products: 364 us -> 0 us
  local copies, waits for them, and re-layouts: 338 us -> 9.78 us
  Pallas kernels: 0 us -> 122 us
  blocking collectives: 42.7 us -> 0 us
  starting transfers between devices: 30.2 us -> 0 us
    unnamed x4 -> x0, waiting for transfers between devices: 526 us -> none
    dot_general x357 -> x0, matrix products: 364 us -> none  [the longest x64 113 us: stretch_forward(): within = jnp.einsum('hts,shp->thp', mixing, values, precision=precise)]
    another operation x257 -> x0, other arithmetic: 185 us -> none
    unnamed x9 -> x0, other arithmetic: 140 us -> none
    pallas_call x0 -> x2, Pallas kernels: none -> 122 us  [the longest x1 87.4 us: local(): pl.pallas_call(functools.partial(scan_kernel, wide, dp), out_shape=(jax.S...]
    squeeze x130 -> x0, local copies, waits for them, and re-layouts: 112 us -> none  [the longest x128 112 us: run_sequence(): lax.scan(jax.checkpoint(advance), initial, (split_blocks(values), split_b...]
    unnamed x38 -> x12, local copies, waits for them, and re-layouts: 99.2 us -> 9.78 us
    add_any x64 -> x0, other arithmetic: 76.6 us -> none  [run_sequence(): lax.scan(jax.checkpoint(advance), initial, (split_blocks(values), split_b...]
  transfers between devices with their start and end apart: 7 -> 0, of which waited for: 4 -> 0; matrix products, arithmetic and copies ran while one was open for 15% -> 0% of each run, Pallas kernels for 0% -> 0%
where the time goes in v1:
time: 133 us
  Pallas kernels  122 us (92%)
  local copies, waits for them, and re-layouts  9.78 us (7%)
    pallas_call x1, Pallas kernels, local(): pl.pallas_call(functools.partial(scan_kernel, wide, dp), out_shape=(jax.S...  87.4 us
    pallas_call x1, Pallas kernels, local(): pl.pallas_call(functools.partial(sum_kernel, wide, dp, heads), out_shape=...  35 us
    unnamed x12, local copies, waits for them, and re-layouts  9.78 us

profile of v1, /device:TPU:1, one launch (start us, length us, event | category | flops | bytes accessed | tf_op | source)
XLA Modules:
  0.0 132.8 jit_solution(2831563259921374801)
XLA Ops:
  0.6 2.4 %copy.13.wdt_hbm = bf16[4096,64]{1,0:T(8,128)(2,1)} copy(bf16[4096,64]{0,1:T(8,128)(2,1)} %param.11) | data formatting | bytes 1048576 | tf_op args[3]
  3.0 87.4 %scan_backward.1 = (bf16[256,4096]{1,0:T(8,128)(2,1)}, bf16[256,4096]{1,0:T(8,128)(2,1)}, bf16[2,64,96,128]{3,2,1,0:T(8,128)(2,1)}) custom-call(bf16[256,4096]{1,0:T(8,128)(2,1)} %bitcast.10, bf16[256,4096]{1,0:T(8,128)(2,1)} %bitcast.11, bf16[256,4096]{1,0:T(8,128)(2,1)} %bitcast.12, bf16[4096,256]{1,0:T(8,128)(2,1)} %wbc_hbm.1, ...), custom_call_target="tpu_custom_call" | custom-call | flops 8053063680 | bytes 8388608 | tf_op jit(solution)/shard_map/scan_backward/pallas_call | solution.py:479
  90.4 0.0 copy-start
  90.4 1.9 %copy-done = bf16[2,64,96,128]{3,2,1,0:T(8,128)(2,1)S(1)} copy-done((bf16[2,64,96,128]{3,2,1,0:T(8,128)(2,1)S(1)}, bf16[2,64,96,128]{3,2,1,0:T(8,128)(2,1)}, u32[]{:S(2)}) %copy-start) | copy-done | bytes 3145752
  92.3 0.0 copy-start.2
  92.3 35.0 %weight_sums.1 = (f32[32,256]{1,0:T(8,128)S(1)}, f32[32,64]{1,0:T(8,128)S(1)}, f32[3,2]{1,0:T(4,128)S(1)}) custom-call(bf16[2,64,96,128]{3,2,1,0:T(8,128)(2,1)S(1)} %copy-done), custom_call_target="tpu_custom_call" | custom-call | tf_op jit(solution)/shard_map/weight_sums/pallas_call | solution.py:530
  127.3 0.6 copy.14
  127.9 0.0 copy-done.2
  127.9 0.0 copy-start.1
  127.9 1.3 copy.19
  129.3 1.0 copy-done.1
  130.3 1.3 copy.20
  131.6 0.6 copy.21
  132.2 0.6 copy.22
Async XLA Ops:
  90.4 1.9 %copy-start = (bf16[2,64,96,128]{3,2,1,0:T(8,128)(2,1)S(1)}, bf16[2,64,96,128]{3,2,1,0:T(8,128)(2,1)}, u32[]{:S(2)}) copy-start(bf16[2,64,96,128]{3,2,1,0:T(8,128)(2,1)} %get-tuple-element.13.wpart_ref) | copy-start | bytes 9437188
  92.3 35.7 %copy-start.2 = (bf16[256,4096]{1,0:T(8,128)(2,1)S(1)}, bf16[256,4096]{1,0:T(8,128)(2,1)}, u32[]{:S(2)}) copy-start(bf16[256,4096]{1,0:T(8,128)(2,1)} %get-tuple-element.11) | copy-start | bytes 6291460
  127.9 2.3 %copy-start.1 = (bf16[256,4096]{1,0:T(8,128)(2,1)S(1)}, bf16[256,4096]{1,0:T(8,128)(2,1)}, u32[]{:S(2)}) copy-start(bf16[256,4096]{1,0:T(8,128)(2,1)} %get-tuple-element.12) | copy-start | bytes 6291460

commit v2 on v1

v2 whole, which is shorter than its diff:
```python
import functools

import jax
import jax.numpy as jnp
from jax import lax
from jax.experimental import pallas as pl
from jax.experimental.pallas import tpu as pltpu
from jax.sharding import PartitionSpec as P

MESH = pl.DeviceIdType.MESH
BF = jnp.bfloat16
F32 = jnp.float32
LANES = 128
BLOCK = 512
STRIDE = 13


def mm(a, b):
    return jnp.dot(a, b, preferred_element_type=F32)


def mm_nt(a, b):
    return lax.dot_general(a, b, (((1,), (1,)), ((), ())), preferred_element_type=F32)


def split2(v):
    hi = v.astype(BF)
    return hi, (v - hi.astype(F32)).astype(BF)


def split3(v):
    hi = v.astype(BF)
    rest = v - hi.astype(F32)
    mid = rest.astype(BF)
    return hi, mid, (rest - mid.astype(F32)).astype(BF)


def scan_kernel(
    wide, dp, in_hbm, x_hbm, g_hbm, wbc_hbm, wdt_hbm, alog_ref, bias_ref, skip_ref,
    xg_hbm, ig_hbm, wbc_out, wdt_out, head_out,
    in_ref, x_ref, g_ref, wbc_ref, wdt_ref, f_ref, gt_ref, gotf_ref, gotg_ref, h_ref, p_ref,
    goth_ref, gotp_ref, xs_ref, gs_ref, gxw_ref, int_ref, sib_ref, nt_ref, st_ref, lt_ref, rt_ref,
    col_ref, hrow_ref, xo_ref, io_ref, dproj_ref, sibd_ref, hg_ref, hsib_ref, ha_ref, hb_ref,
    out_ref, got_ref,
    load_sem, store_sem, sib_send, sib_recv, hs_sem, hr_sem,
    sf_sem, rf_sem, sg_sem, rg_sem, sh_sem, rh_sem, sp_sem, rp_sem, sw_sem, rw_sem,
):
    me = lax.axis_index("wide")
    place = lax.axis_index("dp")
    core = lax.rem(place, 2)
    other = 1 - core
    sets = dp // 2
    slots = wide * sets
    mine = me * sets + place // 2
    seq, width = in_ref.shape
    heads = alog_ref.shape[1]
    half = seq // 2
    nst = wbc_ref.shape[1] // 2
    owners = BLOCK // LANES
    blocks = width // BLOCK
    per_block = BLOCK // 64
    pairs = width // LANES
    group = 8
    groups = slots // group
    sibling = {"wide": me, "dp": place - core + other}

    def at_slot(slot):
        return {"wide": slot // sets, "dp": lax.rem(slot, sets) * 2 + core}

    def to_peer(k):
        return lax.rem(me + k * STRIDE, wide)

    def from_peer(k):
        return lax.rem(me + (wide - k) * STRIDE, wide)

    barrier = pltpu.get_barrier_semaphore()
    pl.semaphore_signal(barrier, inc=1, device_id=sibling, device_id_type=MESH)

    def greet(k, _):
        pl.semaphore_signal(
            barrier, inc=1, device_id=at_slot(lax.rem(mine + k, slots)), device_id_type=MESH
        )
        return 0

    lax.fori_loop(1, slots, greet, 0)

    loads = [
        pltpu.make_async_copy(src, dst, load_sem.at[i])
        for i, (src, dst) in enumerate(
            ((in_hbm, in_ref), (wbc_hbm, wbc_ref), (wdt_hbm, wdt_ref), (x_hbm, x_ref), (g_hbm, g_ref))
        )
    ]
    for load in loads:
        load.start()

    delta = lax.rem(
        lax.broadcasted_iota(jnp.int32, (2 * heads, BLOCK), 0), heads
    ) - lax.broadcasted_iota(jnp.int32, (2 * heads, BLOCK), 1) // 64

    def spread(j):
        return (delta == j * per_block).astype(BF)

    def remote(src, dst, send, recv, target):
        return pltpu.make_async_remote_copy(
            src_ref=src, dst_ref=dst, send_sem=send, recv_sem=recv, device_id=target,
            device_id_type=MESH,
        )

    def send_f(peer):
        return remote(f_ref.at[peer], gotf_ref.at[me], sf_sem.at[peer], rf_sem.at[me], {"wide": peer})

    def send_g(peer):
        return remote(gt_ref.at[peer], gotg_ref.at[me], sg_sem.at[peer], rg_sem.at[me], {"wide": peer})

    def send_h(peer):
        return remote(h_ref.at[peer], goth_ref.at[me], sh_sem.at[peer], rh_sem.at[me], {"wide": peer})

    def send_p(peer):
        return remote(p_ref.at[peer], gotp_ref.at[me], sp_sem.at[peer], rp_sem.at[me], {"wide": peer})

    def send_w(slot):
        return remote(out_ref.at[slot], got_ref.at[mine], sw_sem.at[slot], rw_sem.at[mine], at_slot(slot))

    sib_in = remote(int_ref.at[other], sib_ref, sib_send.at[0], sib_recv.at[0], sibling)
    sib_d = remote(dproj_ref, sibd_ref, sib_send.at[1], sib_recv.at[1], sibling)
    sib_h = remote(hg_ref, hsib_ref, sib_send.at[2], sib_recv.at[2], sibling)

    loads[0].wait()
    loads[1].wait()
    bc = mm(in_ref[...], wbc_ref[...]).astype(BF)
    loads[2].wait()
    dt_raw = mm_nt(in_ref[...], wdt_ref[...]).astype(BF).astype(F32)
    b_rows = bc[:, :nst]
    c_rows = bc[:, nst:]
    b_t = b_rows.astype(F32).T.astype(BF)
    c_t = c_rows.astype(F32).T.astype(BF)
    dt_pre = dt_raw + bias_ref[...]
    dt = jnp.maximum(dt_pre, 0.0) + jnp.log1p(jnp.exp(-jnp.abs(dt_pre)))
    rate = -jnp.exp(alog_ref[...])
    log_rate = dt * rate
    pos_r = lax.broadcasted_iota(jnp.int32, (seq, seq), 0)
    pos_c = lax.broadcasted_iota(jnp.int32, (seq, seq), 1)
    lower = (pos_r >= pos_c).astype(BF)
    lr_hi, lr_mid, lr_lo = split3(log_rate)
    cumul = mm(lower, lr_hi) + mm(lower, lr_mid) + mm(lower, lr_lo)
    last = cumul[seq - 1 :, :]
    tail = dt * jnp.exp(last - cumul)
    tail2 = jnp.concatenate(split2(tail), axis=1)
    lq_hi, lq_mid, lq_lo = split3(last)
    none = jnp.zeros((1, heads), BF)
    lq_rows = jnp.concatenate(
        [jnp.concatenate([v, none], axis=1) for v in (lq_hi, lq_mid, lq_lo)]
        + [jnp.zeros((13, 2 * heads), BF)],
        axis=0,
    )

    def block_at(step):
        return lax.rem(me // owners + (step + 1) * 5, blocks)

    loads[3].wait()
    pl.semaphore_wait(barrier, slots)

    def fresh_f(step, _):
        j = block_at(step)
        cols = pl.ds(pl.multiple_of(j * BLOCK, BLOCK), BLOCK)
        r = spread(j)
        xs = (x_ref[:, cols].astype(F32) * mm(tail2, r)).astype(BF)
        xs_ref[:, cols] = xs
        f_t = mm(b_t, xs).astype(BF)
        lq = mm(lq_rows, r).astype(BF)
        for i in range(owners):
            lanes = slice(i * LANES, (i + 1) * LANES)
            peer = j * owners + i
            f_ref[peer, :nst, :] = f_t[:, lanes]
            f_ref[peer, nst:, :] = lq[:, lanes]

            @pl.when(peer != me)
            def _():
                send_f(peer).start()

        return 0

    lax.fori_loop(0, blocks, fresh_f, 0)

    head_exp = jnp.exp(cumul)
    exp2 = jnp.concatenate(split2(head_exp), axis=1)
    loads[4].wait()

    def fresh_g(step, _):
        j = block_at(step)
        cols = pl.ds(pl.multiple_of(j * BLOCK, BLOCK), BLOCK)
        gs = (g_ref[:, cols].astype(F32) * mm(exp2, spread(j))).astype(BF)
        gs_ref[:, cols] = gs
        g_t = mm(c_t, gs).astype(BF)
        for i in range(owners):
            peer = j * owners + i
            gt_ref[peer] = g_t[:, i * LANES : (i + 1) * LANES]

            @pl.when(peer != me)
            def _():
                send_g(peer).start()

        return 0

    lax.fori_loop(0, blocks, fresh_g, 0)

    lt_ref[...] = cumul.T
    u3 = jnp.concatenate(split3(jnp.log(jnp.maximum(dt, 1e-37)) - cumul), axis=1)
    st_ref[...] = mm_nt(b_rows, c_rows)
    lane = lax.broadcasted_iota(jnp.int32, (seq, LANES), 1)
    lane_head = lax.broadcasted_iota(jnp.int32, (half, heads), 1)
    upper = lax.broadcasted_iota(jnp.int32, (half, half), 0) <= lax.broadcasted_iota(
        jnp.int32, (half, half), 1
    )
    row_head = lax.rem(lax.broadcasted_iota(jnp.int32, (3 * heads, LANES), 0), heads)
    nt_ref[...] = jnp.zeros_like(nt_ref)
    col_ref[...] = jnp.zeros_like(col_ref)

    def within(pair, _):
        cols = pl.ds(pl.multiple_of(pair * LANES, LANES), LANES)
        xk = x_ref[:, cols]
        gk = g_ref[:, cols]
        total_lo = jnp.zeros((half, LANES), F32)
        total_hi = jnp.zeros((half, LANES), F32)
        for side in range(2):
            h = pair * 2 + side
            mine_lane = (lane < 64) if side == 0 else (lane >= 64)
            xm = jnp.where(mine_lane, xk, jnp.zeros_like(xk))
            gm = jnp.where(mine_lane, gk, jnp.zeros_like(gk))
            u = mm(u3, (row_head == h).astype(BF))
            lt = lt_ref[pl.ds(h, 1), :]
            w0 = mm_nt(xm[:half], gk)
            w1 = mm_nt(xm[half:], gk[half:])
            a00 = jnp.where(upper, jnp.exp(u[:half] + lt[:, :half]), 0.0)
            a01 = jnp.exp(u[:half] + lt[:, half:])
            a11 = jnp.where(upper, jnp.exp(u[half:] + lt[:, half:]), 0.0)
            s00 = st_ref[:half, :half]
            s01 = st_ref[:half, half:]
            s11 = st_ref[half:, half:]
            p00 = a00 * w0[:, :half]
            p01 = a01 * w0[:, half:]
            p11 = a11 * w1
            nt_ref[:half, :half] += p00
            nt_ref[:half, half:] += p01
            nt_ref[half:, half:] += p11
            total_lo += mm((a00 * s00).astype(BF), gm[:half]) + mm((a01 * s01).astype(BF), gm[half:])
            total_hi += mm((a11 * s11).astype(BF), gm[half:])
            z00 = p00 * s00
            z01 = p01 * s01
            z11 = p11 * s11
            rt_ref[h, :, :half] = jnp.sum(z00, axis=0, keepdims=True)
            rt_ref[h, :, half:] = jnp.sum(z01 + z11, axis=0, keepdims=True)
            col_ref[:half, :] += jnp.where(
                lane_head == h, jnp.sum(z00 + z01, axis=1, keepdims=True), 0.0
            )
            col_ref[half:, :] += jnp.where(
                lane_head == h, jnp.sum(z11, axis=1, keepdims=True), 0.0
            )
        gxw_ref[:half, cols] = total_lo
        gxw_ref[half:, cols] = total_hi
        turned = in_ref[:, cols].astype(F32).T.astype(BF)
        for i in range(dp):
            int_ref[i % 2, pair * sets + i // 2] = turned[i * 32 : (i + 1) * 32]
        return 0

    first_part = (pairs * 5) // 8
    lax.fori_loop(0, first_part, within, 0)

    def decay_of(i):
        parts = gotf_ref[i, nst:, :].astype(F32)
        return jnp.exp(parts[0:1] + parts[1:2] + parts[2:3])

    def take_f(k, _):
        peer = from_peer(k)
        pltpu.make_async_copy(f_ref.at[peer], gotf_ref.at[peer], rf_sem.at[peer]).wait()
        return 0

    gotf_ref[me] = f_ref[me]
    lax.fori_loop(1, wide, take_f, 0)

    def advance_f(i, state):
        h_ref[i] = state.astype(BF)
        return state * decay_of(i) + gotf_ref[i, :nst, :].astype(F32)

    start = jnp.zeros((nst, LANES), F32)
    lax.fori_loop(0, wide, advance_f, start)

    def give_h(k, _):
        send_h(to_peer(k)).start()
        return 0

    lax.fori_loop(1, wide, give_h, 0)
    goth_ref[me] = h_ref[me]

    lax.fori_loop(first_part, pairs, within, 0)
    sib_in.start()

    def take_g(k, _):
        peer = from_peer(k)
        pltpu.make_async_copy(gt_ref.at[peer], gotg_ref.at[peer], rg_sem.at[peer]).wait()
        return 0

    gotg_ref[me] = gt_ref[me]
    lax.fori_loop(1, wide, take_g, 0)

    def advance_g(k, pull):
        i = wide - 1 - k
        p_ref[i] = pull.astype(BF)
        return pull * decay_of(i) + gotg_ref[i].astype(F32)

    lax.fori_loop(0, wide, advance_g, start)

    def give_p(k, _):
        send_p(to_peer(k)).start()
        return 0

    lax.fori_loop(1, wide, give_p, 0)
    gotp_ref[me] = p_ref[me]

    n_low = nt_ref[...].astype(BF)
    g_b = mm(n_low, c_rows)
    g_c = mm(nt_ref[...].T.astype(BF), b_rows)

    skip_hi, skip_lo = split2(skip_ref[...])
    skip_rows = jnp.concatenate(
        [jnp.concatenate([skip_hi, skip_lo], axis=1)]
        + [jnp.concatenate([v, none], axis=1) for v in (lq_hi, lq_mid, lq_lo)]
        + [jnp.zeros((12, 2 * heads), BF)],
        axis=0,
    )
    narrow = lax.rem(
        lax.broadcasted_iota(jnp.int32, (2 * heads, LANES), 0), heads
    ) - lax.broadcasted_iota(jnp.int32, (2 * heads, LANES), 1) // 64
    gather_delta = lax.broadcasted_iota(jnp.int32, (LANES, heads), 1) - lax.broadcasted_iota(
        jnp.int32, (LANES, heads), 0
    ) // 64

    def finish_f(p, carried):
        row_st, gc = carried
        cols = pl.ds(pl.multiple_of(p * LANES, LANES), LANES)
        gather = (gather_delta == 2 * p).astype(BF)
        h0 = goth_ref[p]
        gs = gs_ref[:, cols]
        y_st = mm(c_rows, h0)
        row_st += mm((gs.astype(F32) * y_st).astype(BF), gather)
        gc += mm_nt(gs, h0)
        hrow_ref[1:2, cols] = jnp.sum(
            x_ref[:, cols].astype(F32) * g_ref[:, cols].astype(F32), axis=0, keepdims=True
        )
        return row_st, gc

    def use_f(k, carried):
        peer = from_peer(k)
        pltpu.make_async_copy(h_ref.at[peer], goth_ref.at[peer], rh_sem.at[peer]).wait()
        return finish_f(peer, carried)

    zero_h = jnp.zeros((seq, heads), F32)
    row_st, g_c = lax.fori_loop(1, wide, use_f, finish_f(me, (zero_h, g_c)))

    def finish_g(p, carried):
        col_st, gb = carried
        cols = pl.ds(pl.multiple_of(p * LANES, LANES), LANES)
        r = (narrow == 2 * p).astype(BF)
        gather = (gather_delta == 2 * p).astype(BF)
        dh = gotp_ref[p]
        xs = xs_ref[:, cols]
        u_st = mm(b_rows, dh)
        rows = mm(skip_rows, r)
        gx = gxw_ref[:, cols] + mm(tail2, r) * u_st + rows[0:1] * g_ref[:, cols].astype(F32)
        xo_ref[:, cols] = gx.astype(BF)
        col_st += mm((xs.astype(F32) * u_st).astype(BF), gather)
        gb += mm_nt(xs, dh)
        ended = goth_ref[p].astype(F32) * jnp.exp(rows[1:2] + rows[2:3] + rows[3:4])
        ended += f_ref[p, :nst, :].astype(F32)
        hrow_ref[0:1, cols] = jnp.sum(ended * dh.astype(F32), axis=0, keepdims=True)
        pltpu.make_async_copy(xo_ref.at[:, cols], xg_hbm.at[:, cols], store_sem.at[0, p]).start()
        return col_st, gb

    def use_g(k, carried):
        peer = from_peer(k)
        pltpu.make_async_copy(p_ref.at[peer], gotp_ref.at[peer], rp_sem.at[peer]).wait()
        return finish_g(peer, carried)

    col_st, g_b = lax.fori_loop(1, wide, use_g, finish_g(me, (zero_h, g_b)))

    head_of = lax.broadcasted_iota(jnp.int32, (width, heads), 0) // 64
    gather_all = (head_of == lax.broadcasted_iota(jnp.int32, (width, heads), 1)).astype(BF)
    hr_hi, hr_lo = split2(hrow_ref[...])
    sums = mm(hr_hi, gather_all) + mm(hr_lo, gather_all)
    crossing, g_skip = sums[0:1], sums[1:2]

    row_all = rt_ref[:, 0, :].T + row_st
    col_all = col_ref[...] + col_st
    upper_all = (pos_r <= pos_c).astype(BF)
    d_hi, d_mid, d_lo = split3(row_all - col_all)
    d_log = mm(upper_all, d_hi) + mm(upper_all, d_mid) + mm(upper_all, d_lo) + crossing
    gate = 1.0 / (1.0 + jnp.exp(-dt_pre))
    ratio = jnp.where(dt > 0.0, gate / jnp.where(dt > 0.0, dt, 1.0), 1.0)
    g_dt = col_all * ratio + rate * d_log * gate
    d_bc = jnp.concatenate([g_b, g_c], axis=1).astype(BF)
    g_raw = g_dt.astype(BF)
    dproj_ref[:, : 2 * nst] = d_bc
    dproj_ref[:, 2 * nst :] = g_raw
    sib_d.start()
    g_alog = jnp.sum(d_log * log_rate, axis=0, keepdims=True)
    g_bias = jnp.sum(g_dt, axis=0, keepdims=True)
    hg_ref[...] = jnp.zeros_like(hg_ref)
    hg_ref[0:1, :heads] = g_alog
    hg_ref[1:2, :heads] = g_bias
    hg_ref[2:3, :heads] = g_skip
    sib_h.start()

    def emit(j, _):
        cols = pl.ds(pl.multiple_of(j * BLOCK, BLOCK), BLOCK)
        d_in = mm_nt(dproj_ref[:, : 2 * nst], wbc_ref[cols, :]) + mm(
            dproj_ref[:, 2 * nst :], wdt_ref[:, cols]
        )
        io_ref[:, cols] = d_in.astype(BF)
        pltpu.make_async_copy(io_ref.at[:, cols], ig_hbm.at[:, cols], store_sem.at[1, j]).start()
        return 0

    lax.fori_loop(0, blocks // 2, emit, 0)

    sib_in.wait_recv()
    sib_d.wait_recv()

    def weigh(step, _):
        c = lax.rem(mine // group + (step + 1) * 5, groups)
        part = pl.ds(c * group, group)
        ours = int_ref[core, part].reshape(group * 32, seq)
        theirs = sib_ref[part].reshape(group * 32, seq)
        w = mm(ours, dproj_ref[...]) + mm(theirs, sibd_ref[...])
        for i in range(group):
            slot = c * group + i
            at = w[i * 32 : (i + 1) * 32]
            out_ref[slot, 0:32, :] = at[:, :LANES].astype(BF)
            out_ref[slot, 32:64, :] = at[:, LANES : 2 * LANES].astype(BF)
            out_ref[slot, 64:80, : 2 * heads] = jnp.concatenate(
                [at[:16, 2 * LANES :], at[16:, 2 * LANES :]], axis=1
            ).astype(BF)

            @pl.when(slot != mine)
            def _():
                send_w(slot).start()

        return 0

    lax.fori_loop(0, groups, weigh, 0)

    ga, gi = mine // group, lax.rem(mine, group)
    sib_h.wait_recv()
    ha_ref[gi] = hg_ref[...] + hsib_ref[...]

    def send_a(i):
        return remote(ha_ref.at[gi], ha_ref.at[gi], hs_sem.at[0, i], hr_sem.at[0, gi], at_slot(ga * group + i))

    def send_b(i):
        return remote(hb_ref.at[ga], hb_ref.at[ga], hs_sem.at[1, i], hr_sem.at[1, ga], at_slot(i * group + gi))

    def start_a(k, _):
        send_a(lax.rem(gi + k, group)).start()
        return 0

    lax.fori_loop(1, group, start_a, 0)
    lax.fori_loop(blocks // 2, blocks, emit, 0)

    def end_a(k, _):
        i = lax.rem(gi + k, group)
        pltpu.make_async_copy(ha_ref.at[i], ha_ref.at[i], hr_sem.at[0, i]).wait()
        send_a(i).wait_send()
        return 0

    lax.fori_loop(1, group, end_a, 0)
    hb_ref[ga] = jnp.sum(ha_ref[...], axis=0)

    def start_b(k, _):
        send_b(lax.rem(ga + k, groups)).start()
        return 0

    lax.fori_loop(1, groups, start_b, 0)

    def drain(k, _):
        f_peer = to_peer(k)
        send_f(f_peer).wait_send()
        send_g(f_peer).wait_send()
        send_h(f_peer).wait_send()
        send_p(f_peer).wait_send()
        return 0

    lax.fori_loop(1, wide, drain, 0)

    def stored_x(p, _):
        cols = pl.ds(pl.multiple_of(p * LANES, LANES), LANES)
        pltpu.make_async_copy(xo_ref.at[:, cols], xg_hbm.at[:, cols], store_sem.at[0, p]).wait()
        return 0

    lax.fori_loop(0, pairs, stored_x, 0)

    def stored_i(j, _):
        cols = pl.ds(pl.multiple_of(j * BLOCK, BLOCK), BLOCK)
        pltpu.make_async_copy(io_ref.at[:, cols], ig_hbm.at[:, cols], store_sem.at[1, j]).wait()
        return 0

    lax.fori_loop(0, blocks, stored_i, 0)
    sib_in.wait_send()
    sib_d.wait_send()
    sib_h.wait_send()

    def end_b(k, _):
        i = lax.rem(ga + k, groups)
        pltpu.make_async_copy(hb_ref.at[i], hb_ref.at[i], hr_sem.at[1, i]).wait()
        send_b(i).wait_send()
        return 0

    lax.fori_loop(1, groups, end_b, 0)
    rows = jnp.sum(hb_ref[...], axis=0)
    at = lax.broadcasted_iota(jnp.int32, rows.shape, 1)
    per = heads // wide
    for i in range(per):
        picked = jnp.sum(jnp.where(at == me * per + i, rows, 0.0), axis=1, keepdims=True)
        head_out[:, i : i + 1] = picked[:3]

    def total(k, acc):
        slot = lax.rem(mine + (slots - k) * 5, slots)
        pltpu.make_async_copy(out_ref.at[slot], got_ref.at[slot], rw_sem.at[slot]).wait()
        return acc + got_ref[slot].astype(F32)

    acc = lax.fori_loop(1, slots, total, out_ref[mine].astype(F32))
    wbc_out[:, :LANES] = acc[0:32]
    wbc_out[:, LANES:] = acc[32:64]
    wdt_out[0:16, :] = acc[64:80, :heads]
    wdt_out[16:32, :] = acc[64:80, heads : 2 * heads]

    def done(k, _):
        send_w(lax.rem(mine + k, slots)).wait_send()
        return 0

    lax.fori_loop(1, slots, done, 0)


def local(wide, dp, layer_input, inner_acts, w_bc, w_dt, a_log, dt_bias, d_skip, out_grad):
    seq, width = layer_input.shape[1:]
    heads = a_log.shape[0]
    nst = w_bc.shape[1] // 2
    slots = wide * dp // 2
    rows = width // (wide * dp)
    any_spec = pl.BlockSpec(memory_space=pl.ANY)
    vmem = pl.BlockSpec(memory_space=pltpu.VMEM)
    dma = pltpu.SemaphoreType.DMA
    v = pltpu.VMEM
    x_grad, input_grad, wbc_grad, wdt_grad, head_grads = pl.pallas_call(
        functools.partial(scan_kernel, wide, dp),
        out_shape=(
            jax.ShapeDtypeStruct((seq, width), BF),
            jax.ShapeDtypeStruct((seq, width), BF),
            jax.ShapeDtypeStruct((rows, 2 * nst), F32),
            jax.ShapeDtypeStruct((rows, heads), F32),
            jax.ShapeDtypeStruct((3, heads // wide), F32),
        ),
        in_specs=[any_spec] * 5 + [vmem] * 3,
        out_specs=(any_spec, any_spec, vmem, vmem, vmem),
        scratch_shapes=[
            v((seq, width), BF),
            v((seq, width), BF),
            v((seq, width), BF),
            v((width, 2 * nst), BF),
            v((heads, width), BF),
            v((wide, nst + 16, LANES), BF),
            v((wide, nst, LANES), BF),
            v((wide, nst + 16, LANES), BF),
            v((wide, nst, LANES), BF),
            v((wide, nst, LANES), BF),
            v((wide, nst, LANES), BF),
            v((wide, nst, LANES), BF),
            v((wide, nst, LANES), BF),
            v((seq, width), BF),
            v((seq, width), BF),
            v((seq, width), F32),
            v((2, slots, 32, seq), BF),
            v((slots, 32, seq), BF),
            v((seq, seq), F32),
            v((seq, seq), F32),
            v((heads, seq), F32),
            v((heads, 1, seq), F32),
            v((seq, heads), F32),
            v((2, width), F32),
            v((seq, width), BF),
            v((seq, width), BF),
            v((seq, 2 * nst + heads), BF),
            v((seq, 2 * nst + heads), BF),
            v((8, LANES), F32),
            v((8, LANES), F32),
            v((8, 8, LANES), F32),
            v((slots // 8, 8, LANES), F32),
            v((slots, 80, LANES), BF),
            v((slots, 80, LANES), BF),
            dma((5,)),
            dma((2, width // LANES)),
            dma((3,)),
            dma((3,)),
            dma((2, 8)),
            dma((2, 8)),
        ]
        + [dma((wide,))] * 8
        + [dma((slots,))] * 2,
        compiler_params=pltpu.CompilerParams(
            collective_id=0, has_side_effects=True, vmem_limit_bytes=56 * 1024 * 1024
        ),
        cost_estimate=pl.CostEstimate(
            flops=30 * seq * width * 256, bytes_accessed=8 * seq * width, transcendentals=0
        ),
        name="scan_backward",
    )(
        layer_input[0], inner_acts[0], out_grad[0], w_bc, w_dt.T,
        a_log[None], dt_bias[None], d_skip[None],
    )
    return x_grad[None], input_grad[None], wbc_grad, wdt_grad, head_grads


def solution(mesh):
    in_specs = (
        P("dp", "wide", None),
        P("dp", "wide", None),
        P(),
        P(),
        P(),
        P(),
        P(),
        P("dp", "wide", None),
    )
    out_specs = (
        P("dp", "wide", None),
        P("dp", "wide", None),
        P(("wide", "dp"), None),
        P(("wide", "dp"), None),
        P(None, "wide"),
    )
    return jax.shard_map(
        functools.partial(local, mesh.shape["wide"], mesh.shape["dp"]),
        mesh=mesh,
        in_specs=in_specs,
        out_specs=out_specs,
        check_vma=False,
    )
```

time: 133 us -> 114 us (0.86)
  Pallas kernels: 122 us -> 105 us
  local copies, waits for them, and re-layouts: 9.78 us -> 7.14 us
    pallas_call x1 -> x0, Pallas kernels: 35 us -> none  [local(): pl.pallas_call(functools.partial(sum_kernel, wide, dp, heads), out_shape=...]
    pallas_call x1, Pallas kernels: 87.4 us -> 105 us  [local(): pl.pallas_call(functools.partial(scan_kernel, wide, dp), out_shape=(jax.S...]
    unnamed x12 -> x11, local copies, waits for them, and re-layouts: 9.78 us -> 7.14 us
where the time goes in v2:
time: 114 us; the launch traced here: 113 us
  Pallas kernels  105 us (92%)
  local copies, waits for them, and re-layouts  7.14 us (6%)
    pallas_call x1, Pallas kernels, local(): pl.pallas_call(functools.partial(scan_kernel, wide, dp), out_shape=(jax.S...  105 us
    unnamed x11, local copies, waits for them, and re-layouts  7.14 us

profile of v2, /device:TPU:1, one launch (start us, length us, event | category | flops | bytes accessed | tf_op | source)
XLA Modules:
  0.0 113.1 jit_solution(15521589961239357316)
XLA Ops:
  0.6 105.3 %scan_backward.1 = (bf16[256,4096]{1,0:T(8,128)(2,1)}, bf16[256,4096]{1,0:T(8,128)(2,1)}, f32[32,256]{1,0:T(8,128)}, f32[32,64]{1,0:T(8,128)}, f32[3,2]{1,0:T(4,128)}) custom-call(bf16[256,4096]{1,0:T(8,128)(2,1)} %bitcast.11, bf16[256,4096]{1,0:T(8,128)(2,1)} %bitcast.12, bf16[256,4096]{1,0:T(8,128)(2,1)} %bitcast.13, bf16[4096,256]{1,0:T(8,128)(2,1)} %wbc_hbm.1, ...), custom_call_target="tpu_custom_call" | custom-call | flops 8053063680 | bytes 8388608 | tf_op jit(solution)/shard_map/scan_backward/pallas_call | solution.py:551
  106.0 1.3 %copy.13 = f32[3,2]{0,1:T(2,128)} copy(f32[3,2]{1,0:T(4,128)} %get-tuple-element.19) | data formatting | bytes 48
  107.3 0.0 copy-start
  107.3 3.3 %copy.18 = bf16[1,256,4096]{2,1,0:T(8,128)(2,1)} copy(bf16[1,256,4096]{2,1,0:T(8,128)(2,1)} %bitcast.10) | data formatting | bytes 4194304
  110.6 0.0 copy-done
  110.6 0.0 copy-start.1
  110.6 0.0 copy-start.2
  110.6 1.3 %copy.19 = bf16[1,256,4096]{2,1,0:T(8,128)(2,1)} copy(bf16[1,256,4096]{2,1,0:T(8,128)(2,1)S(1)} %bitcast.9) | data formatting | bytes 4194304
  111.9 0.0 copy-done.1
  111.9 0.6 copy.20
  112.5 0.0 copy-done.2
  112.5 0.6 copy.21
Async XLA Ops:
  107.3 3.3 %copy-start = (bf16[256,4096]{1,0:T(8,128)(2,1)S(1)}, bf16[256,4096]{1,0:T(8,128)(2,1)}, u32[]{:S(2)}) copy-start(bf16[256,4096]{1,0:T(8,128)(2,1)} %get-tuple-element.11) | copy-start | bytes 6291460
  110.6 1.3 %copy-start.1 = (f32[32,256]{1,0:T(8,128)S(1)}, f32[32,256]{1,0:T(8,128)}, u32[]{:S(2)}) copy-start(f32[32,256]{1,0:T(8,128)} %get-tuple-element.27) | copy-start | bytes 98308
  110.6 1.9 %copy-start.2 = (f32[32,64]{1,0:T(8,128)S(1)}, f32[32,64]{1,0:T(8,128)}, u32[]{:S(2)}) copy-start(f32[32,64]{1,0:T(8,128)} %get-tuple-element.28) | copy-start | bytes 24580

commit v3 on v2

--- a/solution.py
+++ b/solution.py
@@ -256,6 +256,7 @@
             col_ref[half:, :] += jnp.where(
                 lane_head == h, jnp.sum(z11, axis=1, keepdims=True), 0.0
             )
+        hrow_ref[1:2, cols] = jnp.sum(xk.astype(F32) * gk.astype(F32), axis=0, keepdims=True)
         gxw_ref[:half, cols] = total_lo
         gxw_ref[half:, cols] = total_hi
         turned = in_ref[:, cols].astype(F32).T.astype(BF)
@@ -285,11 +286,17 @@
     start = jnp.zeros((nst, LANES), F32)
     lax.fori_loop(0, wide, advance_f, start)
 
-    def give_h(k, _):
-        send_h(to_peer(k)).start()
-        return 0
-
-    lax.fori_loop(1, wide, give_h, 0)
+    def give_h(step, _):
+        for i in range(owners):
+            peer = block_at(step) * owners + i
+
+            @pl.when(peer != me)
+            def _():
+                send_h(peer).start()
+
+        return 0
+
+    lax.fori_loop(0, blocks, give_h, 0)
     goth_ref[me] = h_ref[me]
 
     lax.fori_loop(first_part, pairs, within, 0)
@@ -310,11 +317,17 @@
 
     lax.fori_loop(0, wide, advance_g, start)
 
-    def give_p(k, _):
-        send_p(to_peer(k)).start()
-        return 0
-
-    lax.fori_loop(1, wide, give_p, 0)
+    def give_p(step, _):
+        for i in range(owners):
+            peer = block_at(step) * owners + i
+
+            @pl.when(peer != me)
+            def _():
+                send_p(peer).start()
+
+        return 0
+
+    lax.fori_loop(0, blocks, give_p, 0)
     gotp_ref[me] = p_ref[me]
 
     n_low = nt_ref[...].astype(BF)
@@ -328,41 +341,52 @@
         + [jnp.zeros((12, 2 * heads), BF)],
         axis=0,
     )
-    narrow = lax.rem(
-        lax.broadcasted_iota(jnp.int32, (2 * heads, LANES), 0), heads
-    ) - lax.broadcasted_iota(jnp.int32, (2 * heads, LANES), 1) // 64
-    gather_delta = lax.broadcasted_iota(jnp.int32, (LANES, heads), 1) - lax.broadcasted_iota(
-        jnp.int32, (LANES, heads), 0
+    gather_delta = lax.broadcasted_iota(jnp.int32, (BLOCK, heads), 1) - lax.broadcasted_iota(
+        jnp.int32, (BLOCK, heads), 0
     ) // 64
 
-    def finish_f(p, carried):
+    def block_from(step):
+        return lax.rem(me // owners + (blocks - 1 - step) * 5, blocks)
+
+    def joined(ref, j):
+        return jnp.concatenate([ref[j * owners + i, :nst, :] for i in range(owners)], axis=1)
+
+    def finish_f(step, carried):
         row_st, gc = carried
-        cols = pl.ds(pl.multiple_of(p * LANES, LANES), LANES)
-        gather = (gather_delta == 2 * p).astype(BF)
-        h0 = goth_ref[p]
+        j = block_from(step)
+        for i in range(owners):
+            peer = j * owners + i
+
+            @pl.when(peer != me)
+            def _():
+                pltpu.make_async_copy(h_ref.at[peer], goth_ref.at[peer], rh_sem.at[peer]).wait()
+
+        cols = pl.ds(pl.multiple_of(j * BLOCK, BLOCK), BLOCK)
+        gather = (gather_delta == j * per_block).astype(BF)
+        h0 = joined(goth_ref, j)
         gs = gs_ref[:, cols]
         y_st = mm(c_rows, h0)
         row_st += mm((gs.astype(F32) * y_st).astype(BF), gather)
         gc += mm_nt(gs, h0)
-        hrow_ref[1:2, cols] = jnp.sum(
-            x_ref[:, cols].astype(F32) * g_ref[:, cols].astype(F32), axis=0, keepdims=True
-        )
         return row_st, gc
 
-    def use_f(k, carried):
-        peer = from_peer(k)
-        pltpu.make_async_copy(h_ref.at[peer], goth_ref.at[peer], rh_sem.at[peer]).wait()
-        return finish_f(peer, carried)
-
     zero_h = jnp.zeros((seq, heads), F32)
-    row_st, g_c = lax.fori_loop(1, wide, use_f, finish_f(me, (zero_h, g_c)))
-
-    def finish_g(p, carried):
+    row_st, g_c = lax.fori_loop(0, blocks, finish_f, (zero_h, g_c))
+
+    def finish_g(step, carried):
         col_st, gb = carried
-        cols = pl.ds(pl.multiple_of(p * LANES, LANES), LANES)
-        r = (narrow == 2 * p).astype(BF)
-        gather = (gather_delta == 2 * p).astype(BF)
-        dh = gotp_ref[p]
+        j = block_from(step)
+        for i in range(owners):
+            peer = j * owners + i
+
+            @pl.when(peer != me)
+            def _():
+                pltpu.make_async_copy(p_ref.at[peer], gotp_ref.at[peer], rp_sem.at[peer]).wait()
+
+        cols = pl.ds(pl.multiple_of(j * BLOCK, BLOCK), BLOCK)
+        r = spread(j)
+        gather = (gather_delta == j * per_block).astype(BF)
+        dh = joined(gotp_ref, j)
         xs = xs_ref[:, cols]
         u_st = mm(b_rows, dh)
         rows = mm(skip_rows, r)
@@ -370,18 +394,13 @@
         xo_ref[:, cols] = gx.astype(BF)
         col_st += mm((xs.astype(F32) * u_st).astype(BF), gather)
         gb += mm_nt(xs, dh)
-        ended = goth_ref[p].astype(F32) * jnp.exp(rows[1:2] + rows[2:3] + rows[3:4])
-        ended += f_ref[p, :nst, :].astype(F32)
+        ended = joined(goth_ref, j).astype(F32) * jnp.exp(rows[1:2] + rows[2:3] + rows[3:4])
+        ended += joined(f_ref, j).astype(F32)
         hrow_ref[0:1, cols] = jnp.sum(ended * dh.astype(F32), axis=0, keepdims=True)
-        pltpu.make_async_copy(xo_ref.at[:, cols], xg_hbm.at[:, cols], store_sem.at[0, p]).start()
+        pltpu.make_async_copy(xo_ref.at[:, cols], xg_hbm.at[:, cols], store_sem.at[0, j]).start()
         return col_st, gb
 
-    def use_g(k, carried):
-        peer = from_peer(k)
-        pltpu.make_async_copy(p_ref.at[peer], gotp_ref.at[peer], rp_sem.at[peer]).wait()
-        return finish_g(peer, carried)
-
-    col_st, g_b = lax.fori_loop(1, wide, use_g, finish_g(me, (zero_h, g_b)))
+    col_st, g_b = lax.fori_loop(0, blocks, finish_g, (zero_h, g_b))
 
     head_of = lax.broadcasted_iota(jnp.int32, (width, heads), 0) // 64
     gather_all = (head_of == lax.broadcasted_iota(jnp.int32, (width, heads), 1)).astype(BF)
@@ -489,19 +508,13 @@
 
     lax.fori_loop(1, wide, drain, 0)
 
-    def stored_x(p, _):
-        cols = pl.ds(pl.multiple_of(p * LANES, LANES), LANES)
-        pltpu.make_async_copy(xo_ref.at[:, cols], xg_hbm.at[:, cols], store_sem.at[0, p]).wait()
-        return 0
-
-    lax.fori_loop(0, pairs, stored_x, 0)
-
-    def stored_i(j, _):
+    def stored(j, _):
         cols = pl.ds(pl.multiple_of(j * BLOCK, BLOCK), BLOCK)
+        pltpu.make_async_copy(xo_ref.at[:, cols], xg_hbm.at[:, cols], store_sem.at[0, j]).wait()
         pltpu.make_async_copy(io_ref.at[:, cols], ig_hbm.at[:, cols], store_sem.at[1, j]).wait()
         return 0
 
-    lax.fori_loop(0, blocks, stored_i, 0)
+    lax.fori_loop(0, blocks, stored, 0)
     sib_in.wait_send()
     sib_d.wait_send()
     sib_h.wait_send()
@@ -518,7 +531,8 @@
     per = heads // wide
     for i in range(per):
         picked = jnp.sum(jnp.where(at == me * per + i, rows, 0.0), axis=1, keepdims=True)
-        head_out[:, i : i + 1] = picked[:3]
+        for r in range(3):
+            head_out[i : i + 1, r : r + 1] = picked[r : r + 1]
 
     def total(k, acc):
         slot = lax.rem(mine + (slots - k) * 5, slots)
@@ -536,6 +550,21 @@
         return 0
 
     lax.fori_loop(1, slots, done, 0)
+
+
+def place_kernel(x_in, i_in, b_in, d_in, h_in, x_out, i_out, b_out, d_out, h_out, big, small):
+    copies = []
+    for a, (src, dst) in enumerate(((x_in, x_out), (i_in, i_out))):
+        rows = src.shape[0] // 4
+        for q in range(4):
+            part = pl.ds(q * rows, rows)
+            copies.append(pltpu.make_async_copy(src.at[part], dst.at[part], big.at[a, q]))
+    for a, (src, dst) in enumerate(((b_in, b_out), (d_in, d_out), (h_in, h_out))):
+        copies.append(pltpu.make_async_copy(src, dst, small.at[a]))
+    for c in copies:
+        c.start()
+    for c in copies:
+        c.wait()
 
 
 def local(wide, dp, layer_input, inner_acts, w_bc, w_dt, a_log, dt_bias, d_skip, out_grad):
@@ -555,7 +584,7 @@
             jax.ShapeDtypeStruct((seq, width), BF),
             jax.ShapeDtypeStruct((rows, 2 * nst), F32),
             jax.ShapeDtypeStruct((rows, heads), F32),
-            jax.ShapeDtypeStruct((3, heads // wide), F32),
+            jax.ShapeDtypeStruct((heads // wide, 3), F32),
         ),
         in_specs=[any_spec] * 5 + [vmem] * 3,
         out_specs=(any_spec, any_spec, vmem, vmem, vmem),
@@ -595,7 +624,7 @@
             v((slots, 80, LANES), BF),
             v((slots, 80, LANES), BF),
             dma((5,)),
-            dma((2, width // LANES)),
+            dma((2, width // BLOCK)),
             dma((3,)),
             dma((3,)),
             dma((2, 8)),
@@ -614,7 +643,19 @@
         layer_input[0], inner_acts[0], out_grad[0], w_bc, w_dt.T,
         a_log[None], dt_bias[None], d_skip[None],
     )
-    return x_grad[None], input_grad[None], wbc_grad, wdt_grad, head_grads
+    x_grad, input_grad, wbc_grad, wdt_grad, head_grads = pl.pallas_call(
+        place_kernel,
+        out_shape=tuple(
+            jax.ShapeDtypeStruct(a.shape, a.dtype)
+            for a in (x_grad, input_grad, wbc_grad, wdt_grad, head_grads)
+        ),
+        in_specs=[any_spec] * 5,
+        out_specs=[any_spec] * 5,
+        scratch_shapes=[dma((2, 4)), dma((3,))],
+        compiler_params=pltpu.CompilerParams(vmem_limit_bytes=60 * 1024 * 1024),
+        name="place_results",
+    )(x_grad, input_grad, wbc_grad, wdt_grad, head_grads)
+    return x_grad[None], input_grad[None], wbc_grad, wdt_grad, head_grads.T
 
 
 def solution(mesh):

time: 114 us -> 227 us (1.99)
  Pallas kernels: 105 us -> 226 us
  local copies, waits for them, and re-layouts: 7.14 us -> 0 us
    pallas_call x0 -> x1, Pallas kernels: none -> 130 us  [local(): pl.pallas_call(place_kernel, out_shape=tuple((jax.ShapeDtypeStruct(a.shap...]
    pallas_call x1, Pallas kernels: 105 us -> 96.5 us  [local(): pl.pallas_call(functools.partial(scan_kernel, wide, dp), out_shape=(jax.S...]
    unnamed x11 -> x0, local copies, waits for them, and re-layouts: 7.14 us -> none
where the time goes in v3:
time: 227 us
  Pallas kernels  226 us (100%)
    pallas_call x1, Pallas kernels, local(): pl.pallas_call(place_kernel, out_shape=tuple((jax.ShapeDtypeStruct(a.shap...  130 us
    pallas_call x1, Pallas kernels, local(): pl.pallas_call(functools.partial(scan_kernel, wide, dp), out_shape=(jax.S...  96.5 us

profile of v3, /device:TPU:1, one launch (start us, length us, event | category | flops | bytes accessed | tf_op | source)
XLA Modules:
  0.0 227.0 jit_solution(15440345122362306197)
XLA Ops:
  0.6 96.5 %scan_backward.1 = (bf16[256,4096]{1,0:T(8,128)(2,1)}, bf16[256,4096]{1,0:T(8,128)(2,1)}, f32[32,256]{1,0:T(8,128)}, f32[32,64]{1,0:T(8,128)}, f32[2,3]{1,0:T(2,128)}) custom-call(bf16[256,4096]{1,0:T(8,128)(2,1)} %bitcast.10, bf16[256,4096]{1,0:T(8,128)(2,1)} %bitcast.11, bf16[256,4096]{1,0:T(8,128)(2,1)} %bitcast.12, bf16[4096,256]{1,0:T(8,128)(2,1)} %wbc_hbm.1, ...), custom_call_target="tpu_custom_call" | custom-call | flops 8053063680 | bytes 8388608 | tf_op jit(solution)/shard_map/scan_backward/pallas_call | solution.py:580
  97.2 129.8 %place_results.1 = (bf16[256,4096]{1,0:T(8,128)(2,1)}, bf16[256,4096]{1,0:T(8,128)(2,1)}, f32[32,256]{1,0:T(8,128)}, f32[32,64]{1,0:T(8,128)}, f32[2,3]{1,0:T(2,128)}) custom-call(bf16[256,4096]{1,0:T(8,128)(2,1)} %get-tuple-element.15.x_in, bf16[256,4096]{1,0:T(8,128)(2,1)} %get-tuple-element.16.i_in, f32[32,256]{1,0:T(8,128)} %get-tuple-element.17.b_in, ...), custom_call_target="tpu_custom_call" | custom-call | tf_op jit(solution)/shard_map/place_results/pallas_call | solution.py:646

commit v4 on v2

--- a/solution.py
+++ b/solution.py
@@ -13,6 +13,8 @@
 LANES = 128
 BLOCK = 512
 STRIDE = 13
+STRIDE_W = 27
+PIECES = 8
 
 
 def mm(a, b):
@@ -40,10 +42,10 @@
     xg_hbm, ig_hbm, wbc_out, wdt_out, head_out,
     in_ref, x_ref, g_ref, wbc_ref, wdt_ref, f_ref, gt_ref, gotf_ref, gotg_ref, h_ref, p_ref,
     goth_ref, gotp_ref, xs_ref, gs_ref, gxw_ref, int_ref, sib_ref, nt_ref, st_ref, lt_ref, rt_ref,
-    col_ref, hrow_ref, xo_ref, io_ref, dproj_ref, sibd_ref, hg_ref, hsib_ref, ha_ref, hb_ref,
-    out_ref, got_ref,
+    col_ref, hrow_ref, xo_ref, io_ref, mine_c, mine_b, mine_d, sib_c, sib_b, sib_d,
+    hg_ref, hsib_ref, ha_ref, hb_ref, out_c, out_b, out_d, got_c, got_b, got_d,
     load_sem, store_sem, sib_send, sib_recv, hs_sem, hr_sem,
-    sf_sem, rf_sem, sg_sem, rg_sem, sh_sem, rh_sem, sp_sem, rp_sem, sw_sem, rw_sem,
+    sf_sem, rf_sem, sg_sem, rg_sem, sh_sem, rh_sem, sp_sem, rp_sem, swc_sem, rwc_sem, swb_sem, rwb_sem, swd_sem, rwd_sem,
 ):
     me = lax.axis_index("wide")
     place = lax.axis_index("dp")
@@ -73,6 +75,21 @@
     def from_peer(k):
         return lax.rem(me + (wide - k) * STRIDE, wide)
 
+    def targets(step):
+        return [to_peer(step * owners + i + 1) for i in range(owners)]
+
+    def sources(step):
+        return [from_peer(step * owners + i + 1) for i in range(owners)]
+
+    def lanes_of(p):
+        return pl.ds(pl.multiple_of(p * LANES, LANES), LANES)
+
+    def columns(ref, peers):
+        return jnp.concatenate([ref[:, lanes_of(p)] for p in peers], axis=1)
+
+    def joined(ref, peers):
+        return jnp.concatenate([ref[p, :nst, :] for p in peers], axis=1)
+
     barrier = pltpu.get_barrier_semaphore()
     pl.semaphore_signal(barrier, inc=1, device_id=sibling, device_id_type=MESH)
 
@@ -84,21 +101,35 @@
 
     lax.fori_loop(1, slots, greet, 0)
 
-    loads = [
-        pltpu.make_async_copy(src, dst, load_sem.at[i])
-        for i, (src, dst) in enumerate(
-            ((in_hbm, in_ref), (wbc_hbm, wbc_ref), (wdt_hbm, wdt_ref), (x_hbm, x_ref), (g_hbm, g_ref))
-        )
-    ]
+    quarter = width // 4
+    loads = []
+    for q in range(4):
+        part = pl.ds(q * quarter, quarter)
+        loads.append((
+            pltpu.make_async_copy(in_hbm.at[:, part], in_ref.at[:, part], load_sem.at[0, q]),
+            pltpu.make_async_copy(wbc_hbm.at[part], wbc_ref.at[part], load_sem.at[1, q]),
+            pltpu.make_async_copy(wdt_hbm.at[:, part], wdt_ref.at[:, part], load_sem.at[2, q]),
+        ))
+    load_x = pltpu.make_async_copy(x_hbm, x_ref, load_sem.at[3, 0])
+    load_g = pltpu.make_async_copy(g_hbm, g_ref, load_sem.at[3, 1])
     for load in loads:
-        load.start()
-
-    delta = lax.rem(
-        lax.broadcasted_iota(jnp.int32, (2 * heads, BLOCK), 0), heads
-    ) - lax.broadcasted_iota(jnp.int32, (2 * heads, BLOCK), 1) // 64
-
-    def spread(j):
-        return (delta == j * per_block).astype(BF)
+        for one in load:
+            one.start()
+    load_x.start()
+    load_g.start()
+
+    narrow = lax.rem(
+        lax.broadcasted_iota(jnp.int32, (2 * heads, LANES), 0), heads
+    ) - lax.broadcasted_iota(jnp.int32, (2 * heads, LANES), 1) // 64
+    gather_delta = lax.broadcasted_iota(jnp.int32, (LANES, heads), 1) - lax.broadcasted_iota(
+        jnp.int32, (LANES, heads), 0
+    ) // 64
+
+    def spread(peers):
+        return jnp.concatenate([(narrow == 2 * p).astype(BF) for p in peers], axis=1)
+
+    def gathered(peers):
+        return jnp.concatenate([(gather_delta == 2 * p).astype(BF) for p in peers], axis=0)
 
     def remote(src, dst, send, recv, target):
         return pltpu.make_async_remote_copy(
@@ -118,18 +149,25 @@
     def send_p(peer):
         return remote(p_ref.at[peer], gotp_ref.at[me], sp_sem.at[peer], rp_sem.at[me], {"wide": peer})
 
-    def send_w(slot):
-        return remote(out_ref.at[slot], got_ref.at[mine], sw_sem.at[slot], rw_sem.at[mine], at_slot(slot))
+    def send_w(out, got, send, recv, slot):
+        return remote(out.at[slot], got.at[mine], send.at[slot], recv.at[mine], at_slot(slot))
 
     sib_in = remote(int_ref.at[other], sib_ref, sib_send.at[0], sib_recv.at[0], sibling)
-    sib_d = remote(dproj_ref, sibd_ref, sib_send.at[1], sib_recv.at[1], sibling)
-    sib_h = remote(hg_ref, hsib_ref, sib_send.at[2], sib_recv.at[2], sibling)
-
-    loads[0].wait()
-    loads[1].wait()
-    bc = mm(in_ref[...], wbc_ref[...]).astype(BF)
-    loads[2].wait()
-    dt_raw = mm_nt(in_ref[...], wdt_ref[...]).astype(BF).astype(F32)
+    sibling_c = remote(mine_c, sib_c, sib_send.at[1], sib_recv.at[1], sibling)
+    sibling_b = remote(mine_b, sib_b, sib_send.at[2], sib_recv.at[2], sibling)
+    sibling_d = remote(mine_d, sib_d, sib_send.at[3], sib_recv.at[3], sibling)
+    sib_h = remote(hg_ref, hsib_ref, sib_send.at[4], sib_recv.at[4], sibling)
+
+    bc = jnp.zeros((seq, 2 * nst), F32)
+    dt_raw = jnp.zeros((seq, heads), F32)
+    for q, load in enumerate(loads):
+        for one in load:
+            one.wait()
+        part = slice(q * quarter, (q + 1) * quarter)
+        bc += mm(in_ref[:, part], wbc_ref[part, :])
+        dt_raw += mm_nt(in_ref[:, part], wdt_ref[:, part])
+    bc = bc.astype(BF)
+    dt_raw = dt_raw.astype(BF).astype(F32)
     b_rows = bc[:, :nst]
     c_rows = bc[:, nst:]
     b_t = b_rows.astype(F32).T.astype(BF)
@@ -154,23 +192,18 @@
         axis=0,
     )
 
-    def block_at(step):
-        return lax.rem(me // owners + (step + 1) * 5, blocks)
-
-    loads[3].wait()
+    load_x.wait()
     pl.semaphore_wait(barrier, slots)
 
     def fresh_f(step, _):
-        j = block_at(step)
-        cols = pl.ds(pl.multiple_of(j * BLOCK, BLOCK), BLOCK)
-        r = spread(j)
-        xs = (x_ref[:, cols].astype(F32) * mm(tail2, r)).astype(BF)
-        xs_ref[:, cols] = xs
+        peers = targets(step)
+        r = spread(peers)
+        xs = (columns(x_ref, peers).astype(F32) * mm(tail2, r)).astype(BF)
         f_t = mm(b_t, xs).astype(BF)
         lq = mm(lq_rows, r).astype(BF)
-        for i in range(owners):
+        for i, peer in enumerate(peers):
             lanes = slice(i * LANES, (i + 1) * LANES)
-            peer = j * owners + i
+            xs_ref[:, lanes_of(peer)] = xs[:, lanes]
             f_ref[peer, :nst, :] = f_t[:, lanes]
             f_ref[peer, nst:, :] = lq[:, lanes]
 
@@ -184,17 +217,16 @@
 
     head_exp = jnp.exp(cumul)
     exp2 = jnp.concatenate(split2(head_exp), axis=1)
-    loads[4].wait()
+    load_g.wait()
 
     def fresh_g(step, _):
-        j = block_at(step)
-        cols = pl.ds(pl.multiple_of(j * BLOCK, BLOCK), BLOCK)
-        gs = (g_ref[:, cols].astype(F32) * mm(exp2, spread(j))).astype(BF)
-        gs_ref[:, cols] = gs
+        peers = targets(step)
+        gs = (columns(g_ref, peers).astype(F32) * mm(exp2, spread(peers))).astype(BF)
         g_t = mm(c_t, gs).astype(BF)
-        for i in range(owners):
-            peer = j * owners + i
-            gt_ref[peer] = g_t[:, i * LANES : (i + 1) * LANES]
+        for i, peer in enumerate(peers):
+            lanes = slice(i * LANES, (i + 1) * LANES)
+            gs_ref[:, lanes_of(peer)] = gs[:, lanes]
+            gt_ref[peer] = g_t[:, lanes]
 
             @pl.when(peer != me)
             def _():
@@ -256,6 +288,7 @@
             col_ref[half:, :] += jnp.where(
                 lane_head == h, jnp.sum(z11, axis=1, keepdims=True), 0.0
             )
+        hrow_ref[:, cols] = jnp.sum(xk.astype(F32) * gk.astype(F32), axis=0, keepdims=True)
         gxw_ref[:half, cols] = total_lo
         gxw_ref[half:, cols] = total_hi
         turned = in_ref[:, cols].astype(F32).T.astype(BF)
@@ -328,124 +361,122 @@
         + [jnp.zeros((12, 2 * heads), BF)],
         axis=0,
     )
-    narrow = lax.rem(
-        lax.broadcasted_iota(jnp.int32, (2 * heads, LANES), 0), heads
-    ) - lax.broadcasted_iota(jnp.int32, (2 * heads, LANES), 1) // 64
-    gather_delta = lax.broadcasted_iota(jnp.int32, (LANES, heads), 1) - lax.broadcasted_iota(
-        jnp.int32, (LANES, heads), 0
-    ) // 64
-
-    def finish_f(p, carried):
+    def finish_f(step, carried):
         row_st, gc = carried
-        cols = pl.ds(pl.multiple_of(p * LANES, LANES), LANES)
-        gather = (gather_delta == 2 * p).astype(BF)
-        h0 = goth_ref[p]
-        gs = gs_ref[:, cols]
+        peers = sources(step)
+        for peer in peers:
+
+            @pl.when(peer != me)
+            def _():
+                pltpu.make_async_copy(h_ref.at[peer], goth_ref.at[peer], rh_sem.at[peer]).wait()
+
+        h0 = joined(goth_ref, peers)
+        gs = columns(gs_ref, peers)
         y_st = mm(c_rows, h0)
-        row_st += mm((gs.astype(F32) * y_st).astype(BF), gather)
+        row_st += mm((gs.astype(F32) * y_st).astype(BF), gathered(peers))
         gc += mm_nt(gs, h0)
-        hrow_ref[1:2, cols] = jnp.sum(
-            x_ref[:, cols].astype(F32) * g_ref[:, cols].astype(F32), axis=0, keepdims=True
-        )
         return row_st, gc
 
-    def use_f(k, carried):
-        peer = from_peer(k)
-        pltpu.make_async_copy(h_ref.at[peer], goth_ref.at[peer], rh_sem.at[peer]).wait()
-        return finish_f(peer, carried)
-
     zero_h = jnp.zeros((seq, heads), F32)
-    row_st, g_c = lax.fori_loop(1, wide, use_f, finish_f(me, (zero_h, g_c)))
-
-    def finish_g(p, carried):
-        col_st, gb = carried
-        cols = pl.ds(pl.multiple_of(p * LANES, LANES), LANES)
-        r = (narrow == 2 * p).astype(BF)
-        gather = (gather_delta == 2 * p).astype(BF)
-        dh = gotp_ref[p]
-        xs = xs_ref[:, cols]
+    row_st, g_c = lax.fori_loop(0, blocks, finish_f, (zero_h, g_c))
+    mine_c[...] = g_c.astype(BF)
+    sibling_c.start()
+
+    upper_all = (pos_r <= pos_c).astype(BF)
+
+    def suffix(v):
+        hi, mid, lo = split3(v)
+        return mm(upper_all, hi) + mm(upper_all, mid) + mm(upper_all, lo)
+
+    early = suffix(rt_ref[:, 0, :].T + row_st - col_ref[...])
+    gate = 1.0 / (1.0 + jnp.exp(-dt_pre))
+    ratio = jnp.where(dt > 0.0, gate / jnp.where(dt > 0.0, dt, 1.0), 1.0)
+
+    def finish_g(step, carried):
+        col_st, gb, sums = carried
+        peers = sources(step)
+        for peer in peers:
+
+            @pl.when(peer != me)
+            def _():
+                pltpu.make_async_copy(p_ref.at[peer], gotp_ref.at[peer], rp_sem.at[peer]).wait()
+
+        r = spread(peers)
+        gather = gathered(peers)
+        dh = joined(gotp_ref, peers)
+        xs = columns(xs_ref, peers)
         u_st = mm(b_rows, dh)
         rows = mm(skip_rows, r)
-        gx = gxw_ref[:, cols] + mm(tail2, r) * u_st + rows[0:1] * g_ref[:, cols].astype(F32)
-        xo_ref[:, cols] = gx.astype(BF)
+        gx = columns(gxw_ref, peers) + mm(tail2, r) * u_st
+        gx = (gx + rows[0:1] * columns(g_ref, peers).astype(F32)).astype(BF)
         col_st += mm((xs.astype(F32) * u_st).astype(BF), gather)
         gb += mm_nt(xs, dh)
-        ended = goth_ref[p].astype(F32) * jnp.exp(rows[1:2] + rows[2:3] + rows[3:4])
-        ended += f_ref[p, :nst, :].astype(F32)
-        hrow_ref[0:1, cols] = jnp.sum(ended * dh.astype(F32), axis=0, keepdims=True)
-        pltpu.make_async_copy(xo_ref.at[:, cols], xg_hbm.at[:, cols], store_sem.at[0, p]).start()
-        return col_st, gb
-
-    def use_g(k, carried):
-        peer = from_peer(k)
-        pltpu.make_async_copy(p_ref.at[peer], gotp_ref.at[peer], rp_sem.at[peer]).wait()
-        return finish_g(peer, carried)
-
-    col_st, g_b = lax.fori_loop(1, wide, use_g, finish_g(me, (zero_h, g_b)))
-
-    head_of = lax.broadcasted_iota(jnp.int32, (width, heads), 0) // 64
-    gather_all = (head_of == lax.broadcasted_iota(jnp.int32, (width, heads), 1)).astype(BF)
-    hr_hi, hr_lo = split2(hrow_ref[...])
-    sums = mm(hr_hi, gather_all) + mm(hr_lo, gather_all)
-    crossing, g_skip = sums[0:1], sums[1:2]
-
-    row_all = rt_ref[:, 0, :].T + row_st
-    col_all = col_ref[...] + col_st
-    upper_all = (pos_r <= pos_c).astype(BF)
-    d_hi, d_mid, d_lo = split3(row_all - col_all)
-    d_log = mm(upper_all, d_hi) + mm(upper_all, d_mid) + mm(upper_all, d_lo) + crossing
-    gate = 1.0 / (1.0 + jnp.exp(-dt_pre))
-    ratio = jnp.where(dt > 0.0, gate / jnp.where(dt > 0.0, dt, 1.0), 1.0)
-    g_dt = col_all * ratio + rate * d_log * gate
-    d_bc = jnp.concatenate([g_b, g_c], axis=1).astype(BF)
-    g_raw = g_dt.astype(BF)
-    dproj_ref[:, : 2 * nst] = d_bc
-    dproj_ref[:, 2 * nst :] = g_raw
-    sib_d.start()
+        ended = joined(goth_ref, peers).astype(F32) * jnp.exp(rows[1:2] + rows[2:3] + rows[3:4])
+        ended += joined(f_ref, peers).astype(F32)
+        heads_in = jnp.concatenate(
+            [jnp.sum(ended * dh.astype(F32), axis=0, keepdims=True), columns(hrow_ref, peers)], axis=0
+        )
+        hi, lo = split2(heads_in)
+        sums += mm(hi, gather) + mm(lo, gather)
+        for i, peer in enumerate(peers):
+            cols = lanes_of(peer)
+            xo_ref[:, cols] = gx[:, i * LANES : (i + 1) * LANES]
+            pltpu.make_async_copy(xo_ref.at[:, cols], xg_hbm.at[:, cols], store_sem.at[0, peer]).start()
+        return col_st, gb, sums
+
+    def weigh(mine_p, sib_p, out, got, send, recv, packed):
+        def step_of(step, _):
+            order = [lax.rem(mine + (step * group + i + 1) * STRIDE_W, slots) for i in range(group)]
+            ours = jnp.concatenate([int_ref[core, slot] for slot in order], axis=0)
+            theirs = jnp.concatenate([sib_ref[slot] for slot in order], axis=0)
+            w = mm(ours, mine_p[...]) + mm(theirs, sib_p[...])
+            for i, slot in enumerate(order):
+                at = w[i * 32 : (i + 1) * 32]
+                if packed:
+                    out[slot, :, : 2 * heads] = jnp.concatenate([at[:16], at[16:]], axis=1).astype(BF)
+                else:
+                    out[slot] = at.astype(BF)
+
+                @pl.when(slot != mine)
+                def _():
+                    send_w(out, got, send, recv, slot).start()
+
+            return 0
+
+        lax.fori_loop(0, groups, step_of, 0)
+
+    carried = lax.fori_loop(0, blocks // 4, finish_g, (zero_h, g_b, jnp.zeros((2, heads), F32)))
+    sib_in.wait_recv()
+    sibling_c.wait_recv()
+    weigh(mine_c, sib_c, out_c, got_c, swc_sem, rwc_sem, False)
+    col_st, g_b, sums = lax.fori_loop(blocks // 4, blocks, finish_g, carried)
+    mine_b[...] = g_b.astype(BF)
+    sibling_b.start()
+
+    d_log = early - suffix(col_st) + sums[0:1]
+    g_dt = (col_ref[...] + col_st) * ratio + rate * d_log * gate
+    mine_d[...] = g_dt.astype(BF)
+    sibling_d.start()
     g_alog = jnp.sum(d_log * log_rate, axis=0, keepdims=True)
     g_bias = jnp.sum(g_dt, axis=0, keepdims=True)
     hg_ref[...] = jnp.zeros_like(hg_ref)
     hg_ref[0:1, :heads] = g_alog
     hg_ref[1:2, :heads] = g_bias
-    hg_ref[2:3, :heads] = g_skip
+    hg_ref[2:3, :heads] = sums[1:2]
     sib_h.start()
+
+    sibling_b.wait_recv()
+    weigh(mine_b, sib_b, out_b, got_b, swb_sem, rwb_sem, False)
+    sibling_d.wait_recv()
+    weigh(mine_d, sib_d, out_d, got_d, swd_sem, rwd_sem, True)
 
     def emit(j, _):
         cols = pl.ds(pl.multiple_of(j * BLOCK, BLOCK), BLOCK)
-        d_in = mm_nt(dproj_ref[:, : 2 * nst], wbc_ref[cols, :]) + mm(
-            dproj_ref[:, 2 * nst :], wdt_ref[:, cols]
-        )
+        d_in = mm_nt(mine_b[...], wbc_ref[cols, :nst]) + mm_nt(mine_c[...], wbc_ref[cols, nst:])
+        d_in += mm(mine_d[...], wdt_ref[:, cols])
         io_ref[:, cols] = d_in.astype(BF)
         pltpu.make_async_copy(io_ref.at[:, cols], ig_hbm.at[:, cols], store_sem.at[1, j]).start()
         return 0
-
-    lax.fori_loop(0, blocks // 2, emit, 0)
-
-    sib_in.wait_recv()
-    sib_d.wait_recv()
-
-    def weigh(step, _):
-        c = lax.rem(mine // group + (step + 1) * 5, groups)
-        part = pl.ds(c * group, group)
-        ours = int_ref[core, part].reshape(group * 32, seq)
-        theirs = sib_ref[part].reshape(group * 32, seq)
-        w = mm(ours, dproj_ref[...]) + mm(theirs, sibd_ref[...])
-        for i in range(group):
-            slot = c * group + i
-            at = w[i * 32 : (i + 1) * 32]
-            out_ref[slot, 0:32, :] = at[:, :LANES].astype(BF)
-            out_ref[slot, 32:64, :] = at[:, LANES : 2 * LANES].astype(BF)
-            out_ref[slot, 64:80, : 2 * heads] = jnp.concatenate(
-                [at[:16, 2 * LANES :], at[16:, 2 * LANES :]], axis=1
-            ).astype(BF)
-
-            @pl.when(slot != mine)
-            def _():
-                send_w(slot).start()
-
-        return 0
-
-    lax.fori_loop(0, groups, weigh, 0)
 
     ga, gi = mine // group, lax.rem(mine, group)
     sib_h.wait_recv()
@@ -462,7 +493,7 @@
         return 0
 
     lax.fori_loop(1, group, start_a, 0)
-    lax.fori_loop(blocks // 2, blocks, emit, 0)
+    lax.fori_loop(0, blocks, emit, 0)
 
     def end_a(k, _):
         i = lax.rem(gi + k, group)
@@ -490,11 +521,11 @@
     lax.fori_loop(1, wide, drain, 0)
 
     def stored_x(p, _):
-        cols = pl.ds(pl.multiple_of(p * LANES, LANES), LANES)
+        cols = lanes_of(p)
         pltpu.make_async_copy(xo_ref.at[:, cols], xg_hbm.at[:, cols], store_sem.at[0, p]).wait()
         return 0
 
-    lax.fori_loop(0, pairs, stored_x, 0)
+    lax.fori_loop(0, wide, stored_x, 0)
 
     def stored_i(j, _):
         cols = pl.ds(pl.multiple_of(j * BLOCK, BLOCK), BLOCK)
@@ -503,7 +534,9 @@
 
     lax.fori_loop(0, blocks, stored_i, 0)
     sib_in.wait_send()
-    sib_d.wait_send()
+    sibling_c.wait_send()
+    sibling_b.wait_send()
+    sibling_d.wait_send()
     sib_h.wait_send()
 
     def end_b(k, _):
@@ -518,24 +551,58 @@
     per = heads // wide
     for i in range(per):
         picked = jnp.sum(jnp.where(at == me * per + i, rows, 0.0), axis=1, keepdims=True)
-        head_out[:, i : i + 1] = picked[:3]
-
-    def total(k, acc):
-        slot = lax.rem(mine + (slots - k) * 5, slots)
-        pltpu.make_async_copy(out_ref.at[slot], got_ref.at[slot], rw_sem.at[slot]).wait()
-        return acc + got_ref[slot].astype(F32)
-
-    acc = lax.fori_loop(1, slots, total, out_ref[mine].astype(F32))
-    wbc_out[:, :LANES] = acc[0:32]
-    wbc_out[:, LANES:] = acc[32:64]
-    wdt_out[0:16, :] = acc[64:80, :heads]
-    wdt_out[16:32, :] = acc[64:80, heads : 2 * heads]
+        for r in range(3):
+            head_out[i : i + 1, r : r + 1] = picked[r : r + 1]
+
+    def total(out, got, recv, acc):
+        def add(k, acc):
+            slot = lax.rem(mine + (slots - k) * STRIDE_W, slots)
+            pltpu.make_async_copy(out.at[slot], got.at[slot], recv.at[slot]).wait()
+            return acc + got[slot].astype(F32)
+
+        return lax.fori_loop(1, slots, add, acc)
+
+    wbc_out[:, LANES:] = total(out_c, got_c, rwc_sem, out_c[mine].astype(F32))
+    wbc_out[:, :LANES] = total(out_b, got_b, rwb_sem, out_b[mine].astype(F32))
+    acc = total(out_d, got_d, rwd_sem, out_d[mine].astype(F32))
+    wdt_out[0:16, :] = acc[:, :heads]
+    wdt_out[16:32, :] = acc[:, heads : 2 * heads]
 
     def done(k, _):
-        send_w(lax.rem(mine + k, slots)).wait_send()
+        slot = lax.rem(mine + k, slots)
+        send_w(out_c, got_c, swc_sem, rwc_sem, slot).wait_send()
+        send_w(out_b, got_b, swb_sem, rwb_sem, slot).wait_send()
+        send_w(out_d, got_d, swd_sem, rwd_sem, slot).wait_send()
         return 0
 
     lax.fori_loop(1, slots, done, 0)
+
+
+def place_kernel(
+    x_in, i_in, b_in, d_in, h_in, x_out, i_out, b_out, d_out, h_out,
+    x_ref, i_ref, b_ref, d_ref, h_ref, come, go, come_small, go_small,
+):
+    steps = []
+    for a, (src, mid, dst) in enumerate(((b_in, b_ref, b_out), (d_in, d_ref, d_out), (h_in, h_ref, h_out))):
+        steps.append((
+            pltpu.make_async_copy(src, mid, come_small.at[a]),
+            pltpu.make_async_copy(mid, dst, go_small.at[a]),
+        ))
+    for q in range(PIECES):
+        for a, (src, mid, dst) in enumerate(((x_in, x_ref, x_out), (i_in, i_ref, i_out))):
+            rows = src.shape[0] // PIECES
+            part = pl.ds(q * rows, rows)
+            steps.append((
+                pltpu.make_async_copy(src.at[part], mid.at[part], come.at[a, q]),
+                pltpu.make_async_copy(mid.at[part], dst.at[part], go.at[a, q]),
+            ))
+    for first, _ in steps:
+        first.start()
+    for first, second in steps:
+        first.wait()
+        second.start()
+    for _, second in steps:
+        second.wait()
 
 
 def local(wide, dp, layer_input, inner_acts, w_bc, w_dt, a_log, dt_bias, d_skip, out_grad):
@@ -555,7 +622,7 @@
             jax.ShapeDtypeStruct((seq, width), BF),
             jax.ShapeDtypeStruct((rows, 2 * nst), F32),
             jax.ShapeDtypeStruct((rows, heads), F32),
-            jax.ShapeDtypeStruct((3, heads // wide), F32),
+            jax.ShapeDtypeStruct((heads // wide, 3), F32),
         ),
         in_specs=[any_spec] * 5 + [vmem] * 3,
         out_specs=(any_spec, any_spec, vmem, vmem, vmem),
@@ -583,26 +650,34 @@
             v((heads, seq), F32),
             v((heads, 1, seq), F32),
             v((seq, heads), F32),
-            v((2, width), F32),
+            v((1, width), F32),
             v((seq, width), BF),
             v((seq, width), BF),
-            v((seq, 2 * nst + heads), BF),
-            v((seq, 2 * nst + heads), BF),
+            v((seq, nst), BF),
+            v((seq, nst), BF),
+            v((seq, heads), BF),
+            v((seq, nst), BF),
+            v((seq, nst), BF),
+            v((seq, heads), BF),
             v((8, LANES), F32),
             v((8, LANES), F32),
             v((8, 8, LANES), F32),
             v((slots // 8, 8, LANES), F32),
-            v((slots, 80, LANES), BF),
-            v((slots, 80, LANES), BF),
+            v((slots, 32, LANES), BF),
+            v((slots, 32, LANES), BF),
+            v((slots, 16, LANES), BF),
+            v((slots, 32, LANES), BF),
+            v((slots, 32, LANES), BF),
+            v((slots, 16, LANES), BF),
+            dma((4, 4)),
+            dma((2, wide)),
             dma((5,)),
-            dma((2, width // LANES)),
-            dma((3,)),
-            dma((3,)),
+            dma((5,)),
             dma((2, 8)),
             dma((2, 8)),
         ]
         + [dma((wide,))] * 8
-        + [dma((slots,))] * 2,
+        + [dma((slots,))] * 6,
         compiler_params=pltpu.CompilerParams(
             collective_id=0, has_side_effects=True, vmem_limit_bytes=56 * 1024 * 1024
         ),
@@ -614,7 +689,22 @@
         layer_input[0], inner_acts[0], out_grad[0], w_bc, w_dt.T,
         a_log[None], dt_bias[None], d_skip[None],
     )
-    return x_grad[None], input_grad[None], wbc_grad, wdt_grad, head_grads
+    x_grad, input_grad, wbc_grad, wdt_grad, head_grads = pl.pallas_call(
+        place_kernel,
+        out_shape=tuple(
+            jax.ShapeDtypeStruct(a.shape, a.dtype)
+            for a in (x_grad, input_grad, wbc_grad, wdt_grad, head_grads)
+        ),
+        in_specs=[any_spec] * 5,
+        out_specs=[any_spec] * 5,
+        scratch_shapes=[
+            v(a.shape, a.dtype) for a in (x_grad, input_grad, wbc_grad, wdt_grad, head_grads)
+        ]
+        + [dma((2, PIECES)), dma((2, PIECES)), dma((3,)), dma((3,))],
+        compiler_params=pltpu.CompilerParams(vmem_limit_bytes=60 * 1024 * 1024),
+        name="place_results",
+    )(x_grad, input_grad, wbc_grad, wdt_grad, head_grads)
+    return x_grad[None], input_grad[None], wbc_grad, wdt_grad, head_grads.T
 
 
 def solution(mesh):

time: 114 us -> 98.5 us (0.86)
  Pallas kernels: 105 us -> 97.5 us
  local copies, waits for them, and re-layouts: 7.14 us -> 0 us
    pallas_call x1, Pallas kernels: 105 us -> 93.3 us  [local(): pl.pallas_call(functools.partial(scan_kernel, wide, dp), out_shape=(jax.S...]
    unnamed x11 -> x0, local copies, waits for them, and re-layouts: 7.14 us -> none
    pallas_call x0 -> x1, Pallas kernels: none -> 4.19 us  [local(): pl.pallas_call(place_kernel, out_shape=tuple((jax.ShapeDtypeStruct(a.shap...]
where the time goes in v4:
time: 98.5 us; the launch traced here: 98.1 us
  Pallas kernels  97.5 us (99%)
    pallas_call x1, Pallas kernels, local(): pl.pallas_call(functools.partial(scan_kernel, wide, dp), out_shape=(jax.S...  93.3 us
    pallas_call x1, Pallas kernels, local(): pl.pallas_call(place_kernel, out_shape=tuple((jax.ShapeDtypeStruct(a.shap...  4.19 us

profile of v4, /device:TPU:1, one launch (start us, length us, event | category | flops | bytes accessed | tf_op | source)
XLA Modules:
  0.0 98.1 jit_solution(8099668760850613087)
XLA Ops:
  0.6 93.3 %scan_backward.1 = (bf16[256,4096]{1,0:T(8,128)(2,1)}, bf16[256,4096]{1,0:T(8,128)(2,1)}, f32[32,256]{1,0:T(8,128)}, f32[32,64]{1,0:T(8,128)}, f32[2,3]{1,0:T(2,128)}) custom-call(bf16[256,4096]{1,0:T(8,128)(2,1)} %bitcast.10, bf16[256,4096]{1,0:T(8,128)(2,1)} %bitcast.11, bf16[256,4096]{1,0:T(8,128)(2,1)} %bitcast.12, bf16[4096,256]{1,0:T(8,128)(2,1)} %wbc_hbm.1, ...), custom_call_target="tpu_custom_call" | custom-call | flops 8053063680 | bytes 8388608 | tf_op jit(solution)/shard_map/scan_backward/pallas_call | solution.py:618
  93.9 4.2 %place_results.1 = (bf16[256,4096]{1,0:T(8,128)(2,1)}, bf16[256,4096]{1,0:T(8,128)(2,1)}, f32[32,256]{1,0:T(8,128)}, f32[32,64]{1,0:T(8,128)}, f32[2,3]{1,0:T(2,128)}) custom-call(bf16[256,4096]{1,0:T(8,128)(2,1)} %get-tuple-element.15.x_in, bf16[256,4096]{1,0:T(8,128)(2,1)} %get-tuple-element.16.i_in, f32[32,256]{1,0:T(8,128)} %get-tuple-element.17.b_in, ...), custom_call_target="tpu_custom_call" | custom-call | tf_op jit(solution)/shard_map/place_results/pallas_call | solution.py:692

commit v5 on v4

--- a/solution.py
+++ b/solution.py
@@ -14,6 +14,7 @@
 BLOCK = 512
 STRIDE = 13
 STRIDE_W = 27
+WEIGHED = 16
 PIECES = 8
 
 
@@ -44,8 +45,8 @@
     goth_ref, gotp_ref, xs_ref, gs_ref, gxw_ref, int_ref, sib_ref, nt_ref, st_ref, lt_ref, rt_ref,
     col_ref, hrow_ref, xo_ref, io_ref, mine_c, mine_b, mine_d, sib_c, sib_b, sib_d,
     hg_ref, hsib_ref, ha_ref, hb_ref, out_c, out_b, out_d, got_c, got_b, got_d,
-    load_sem, store_sem, sib_send, sib_recv, hs_sem, hr_sem,
-    sf_sem, rf_sem, sg_sem, rg_sem, sh_sem, rh_sem, sp_sem, rp_sem, swc_sem, rwc_sem, swb_sem, rwb_sem, swd_sem, rwd_sem,
+    load_sem, store_sem, sib_send, sib_recv,
+    out_sem, in_sem, rh_sem, rp_sem,
 ):
     me = lax.axis_index("wide")
     place = lax.axis_index("dp")
@@ -138,19 +139,36 @@
         )
 
     def send_f(peer):
-        return remote(f_ref.at[peer], gotf_ref.at[me], sf_sem.at[peer], rf_sem.at[me], {"wide": peer})
+        return remote(f_ref.at[peer], gotf_ref.at[me], out_sem.at[0], in_sem.at[0], {"wide": peer})
 
     def send_g(peer):
-        return remote(gt_ref.at[peer], gotg_ref.at[me], sg_sem.at[peer], rg_sem.at[me], {"wide": peer})
-
-    def send_h(peer):
-        return remote(h_ref.at[peer], goth_ref.at[me], sh_sem.at[peer], rh_sem.at[me], {"wide": peer})
-
-    def send_p(peer):
-        return remote(p_ref.at[peer], gotp_ref.at[me], sp_sem.at[peer], rp_sem.at[me], {"wide": peer})
-
-    def send_w(out, got, send, recv, slot):
-        return remote(out.at[slot], got.at[mine], send.at[slot], recv.at[mine], at_slot(slot))
+        return remote(gt_ref.at[peer], gotg_ref.at[me], out_sem.at[1], in_sem.at[1], {"wide": peer})
+
+    def send_h(k):
+        peer = to_peer(k)
+        step = (k - 1) // owners
+        return remote(h_ref.at[peer], goth_ref.at[me], out_sem.at[2], rh_sem.at[step], {"wide": peer})
+
+    def send_p(k):
+        peer = to_peer(k)
+        step = (k - 1) // owners
+        return remote(p_ref.at[peer], gotp_ref.at[me], out_sem.at[3], rp_sem.at[step], {"wide": peer})
+
+    def send_w(out, got, which, slot):
+        return remote(out.at[slot], got.at[mine], out_sem.at[which], in_sem.at[which], at_slot(slot))
+
+    def wait_for(ref, count, sem):
+        part = ref.at[pl.ds(0, count)]
+        pltpu.make_async_copy(part, part, sem).wait()
+
+    def wait_step(ref, sem, step):
+        @pl.when(step < blocks - 1)
+        def _():
+            wait_for(ref, owners, sem.at[step])
+
+        @pl.when(step == blocks - 1)
+        def _():
+            wait_for(ref, owners - 1, sem.at[step])
 
     sib_in = remote(int_ref.at[other], sib_ref, sib_send.at[0], sib_recv.at[0], sibling)
     sibling_c = remote(mine_c, sib_c, sib_send.at[1], sib_recv.at[1], sibling)
@@ -303,13 +321,8 @@
         parts = gotf_ref[i, nst:, :].astype(F32)
         return jnp.exp(parts[0:1] + parts[1:2] + parts[2:3])
 
-    def take_f(k, _):
-        peer = from_peer(k)
-        pltpu.make_async_copy(f_ref.at[peer], gotf_ref.at[peer], rf_sem.at[peer]).wait()
-        return 0
-
     gotf_ref[me] = f_ref[me]
-    lax.fori_loop(1, wide, take_f, 0)
+    wait_for(gotf_ref, wide - 1, in_sem.at[0])
 
     def advance_f(i, state):
         h_ref[i] = state.astype(BF)
@@ -319,7 +332,7 @@
     lax.fori_loop(0, wide, advance_f, start)
 
     def give_h(k, _):
-        send_h(to_peer(k)).start()
+        send_h(k).start()
         return 0
 
     lax.fori_loop(1, wide, give_h, 0)
@@ -328,13 +341,8 @@
     lax.fori_loop(first_part, pairs, within, 0)
     sib_in.start()
 
-    def take_g(k, _):
-        peer = from_peer(k)
-        pltpu.make_async_copy(gt_ref.at[peer], gotg_ref.at[peer], rg_sem.at[peer]).wait()
-        return 0
-
     gotg_ref[me] = gt_ref[me]
-    lax.fori_loop(1, wide, take_g, 0)
+    wait_for(gotg_ref, wide - 1, in_sem.at[1])
 
     def advance_g(k, pull):
         i = wide - 1 - k
@@ -344,7 +352,7 @@
     lax.fori_loop(0, wide, advance_g, start)
 
     def give_p(k, _):
-        send_p(to_peer(k)).start()
+        send_p(k).start()
         return 0
 
     lax.fori_loop(1, wide, give_p, 0)
@@ -364,12 +372,7 @@
     def finish_f(step, carried):
         row_st, gc = carried
         peers = sources(step)
-        for peer in peers:
-
-            @pl.when(peer != me)
-            def _():
-                pltpu.make_async_copy(h_ref.at[peer], goth_ref.at[peer], rh_sem.at[peer]).wait()
-
+        wait_step(goth_ref, rh_sem, step)
         h0 = joined(goth_ref, peers)
         gs = columns(gs_ref, peers)
         y_st = mm(c_rows, h0)
@@ -395,12 +398,7 @@
     def finish_g(step, carried):
         col_st, gb, sums = carried
         peers = sources(step)
-        for peer in peers:
-
-            @pl.when(peer != me)
-            def _():
-                pltpu.make_async_copy(p_ref.at[peer], gotp_ref.at[peer], rp_sem.at[peer]).wait()
-
+        wait_step(gotp_ref, rp_sem, step)
         r = spread(peers)
         gather = gathered(peers)
         dh = joined(gotp_ref, peers)
@@ -421,12 +419,14 @@
         for i, peer in enumerate(peers):
             cols = lanes_of(peer)
             xo_ref[:, cols] = gx[:, i * LANES : (i + 1) * LANES]
-            pltpu.make_async_copy(xo_ref.at[:, cols], xg_hbm.at[:, cols], store_sem.at[0, peer]).start()
+            pltpu.make_async_copy(xo_ref.at[:, cols], xg_hbm.at[:, cols], store_sem.at[0]).start()
         return col_st, gb, sums
 
-    def weigh(mine_p, sib_p, out, got, send, recv, packed):
+    def weigh(mine_p, sib_p, out, got, which, packed):
         def step_of(step, _):
-            order = [lax.rem(mine + (step * group + i + 1) * STRIDE_W, slots) for i in range(group)]
+            order = [
+                lax.rem(mine + (step * WEIGHED + i + 1) * STRIDE_W, slots) for i in range(WEIGHED)
+            ]
             ours = jnp.concatenate([int_ref[core, slot] for slot in order], axis=0)
             theirs = jnp.concatenate([sib_ref[slot] for slot in order], axis=0)
             w = mm(ours, mine_p[...]) + mm(theirs, sib_p[...])
@@ -439,16 +439,16 @@
 
                 @pl.when(slot != mine)
                 def _():
-                    send_w(out, got, send, recv, slot).start()
+                    send_w(out, got, which, slot).start()
 
             return 0
 
-        lax.fori_loop(0, groups, step_of, 0)
+        lax.fori_loop(0, slots // WEIGHED, step_of, 0)
 
     carried = lax.fori_loop(0, blocks // 4, finish_g, (zero_h, g_b, jnp.zeros((2, heads), F32)))
     sib_in.wait_recv()
     sibling_c.wait_recv()
-    weigh(mine_c, sib_c, out_c, got_c, swc_sem, rwc_sem, False)
+    weigh(mine_c, sib_c, out_c, got_c, 4, False)
     col_st, g_b, sums = lax.fori_loop(blocks // 4, blocks, finish_g, carried)
     mine_b[...] = g_b.astype(BF)
     sibling_b.start()
@@ -465,87 +465,56 @@
     hg_ref[2:3, :heads] = sums[1:2]
     sib_h.start()
 
+    ga, gi = mine // group, lax.rem(mine, group)
+
+    def send_a(i):
+        return remote(ha_ref.at[gi], ha_ref.at[gi], out_sem.at[7], in_sem.at[7], at_slot(ga * group + i))
+
+    def send_b(i):
+        return remote(hb_ref.at[ga], hb_ref.at[ga], out_sem.at[8], in_sem.at[8], at_slot(i * group + gi))
+
+    def start_a(k, _):
+        send_a(lax.rem(gi + k, group)).start()
+        return 0
+
+    def start_b(k, _):
+        send_b(lax.rem(ga + k, groups)).start()
+        return 0
+
     sibling_b.wait_recv()
-    weigh(mine_b, sib_b, out_b, got_b, swb_sem, rwb_sem, False)
+    weigh(mine_b, sib_b, out_b, got_b, 5, False)
+    sib_h.wait_recv()
+    ha_ref[gi] = hg_ref[...] + hsib_ref[...]
+    lax.fori_loop(1, group, start_a, 0)
     sibling_d.wait_recv()
-    weigh(mine_d, sib_d, out_d, got_d, swd_sem, rwd_sem, True)
+    weigh(mine_d, sib_d, out_d, got_d, 6, True)
 
     def emit(j, _):
         cols = pl.ds(pl.multiple_of(j * BLOCK, BLOCK), BLOCK)
         d_in = mm_nt(mine_b[...], wbc_ref[cols, :nst]) + mm_nt(mine_c[...], wbc_ref[cols, nst:])
         d_in += mm(mine_d[...], wdt_ref[:, cols])
         io_ref[:, cols] = d_in.astype(BF)
-        pltpu.make_async_copy(io_ref.at[:, cols], ig_hbm.at[:, cols], store_sem.at[1, j]).start()
-        return 0
-
-    ga, gi = mine // group, lax.rem(mine, group)
-    sib_h.wait_recv()
-    ha_ref[gi] = hg_ref[...] + hsib_ref[...]
-
-    def send_a(i):
-        return remote(ha_ref.at[gi], ha_ref.at[gi], hs_sem.at[0, i], hr_sem.at[0, gi], at_slot(ga * group + i))
-
-    def send_b(i):
-        return remote(hb_ref.at[ga], hb_ref.at[ga], hs_sem.at[1, i], hr_sem.at[1, ga], at_slot(i * group + gi))
-
-    def start_a(k, _):
-        send_a(lax.rem(gi + k, group)).start()
-        return 0
-
-    lax.fori_loop(1, group, start_a, 0)
-    lax.fori_loop(0, blocks, emit, 0)
-
-    def end_a(k, _):
-        i = lax.rem(gi + k, group)
-        pltpu.make_async_copy(ha_ref.at[i], ha_ref.at[i], hr_sem.at[0, i]).wait()
-        send_a(i).wait_send()
-        return 0
-
-    lax.fori_loop(1, group, end_a, 0)
+        pltpu.make_async_copy(io_ref.at[:, cols], ig_hbm.at[:, cols], store_sem.at[1]).start()
+        return 0
+
+    lax.fori_loop(0, blocks // 2, emit, 0)
+    wait_for(ha_ref, group - 1, in_sem.at[7])
     hb_ref[ga] = jnp.sum(ha_ref[...], axis=0)
-
-    def start_b(k, _):
-        send_b(lax.rem(ga + k, groups)).start()
-        return 0
-
     lax.fori_loop(1, groups, start_b, 0)
-
-    def drain(k, _):
-        f_peer = to_peer(k)
-        send_f(f_peer).wait_send()
-        send_g(f_peer).wait_send()
-        send_h(f_peer).wait_send()
-        send_p(f_peer).wait_send()
-        return 0
-
-    lax.fori_loop(1, wide, drain, 0)
-
-    def stored_x(p, _):
-        cols = lanes_of(p)
-        pltpu.make_async_copy(xo_ref.at[:, cols], xg_hbm.at[:, cols], store_sem.at[0, p]).wait()
-        return 0
-
-    lax.fori_loop(0, wide, stored_x, 0)
-
-    def stored_i(j, _):
-        cols = pl.ds(pl.multiple_of(j * BLOCK, BLOCK), BLOCK)
-        pltpu.make_async_copy(io_ref.at[:, cols], ig_hbm.at[:, cols], store_sem.at[1, j]).wait()
-        return 0
-
-    lax.fori_loop(0, blocks, stored_i, 0)
+    lax.fori_loop(blocks // 2, blocks, emit, 0)
+
+    for at, ref in enumerate((f_ref, gt_ref, h_ref, p_ref)):
+        wait_for(ref, wide - 1, out_sem.at[at])
+    wait_for(ha_ref, group - 1, out_sem.at[7])
+    pltpu.make_async_copy(xo_ref, xg_hbm, store_sem.at[0]).wait()
+    pltpu.make_async_copy(io_ref, ig_hbm, store_sem.at[1]).wait()
     sib_in.wait_send()
     sibling_c.wait_send()
     sibling_b.wait_send()
     sibling_d.wait_send()
     sib_h.wait_send()
 
-    def end_b(k, _):
-        i = lax.rem(ga + k, groups)
-        pltpu.make_async_copy(hb_ref.at[i], hb_ref.at[i], hr_sem.at[1, i]).wait()
-        send_b(i).wait_send()
-        return 0
-
-    lax.fori_loop(1, groups, end_b, 0)
+    wait_for(hb_ref, groups - 1, in_sem.at[8])
     rows = jnp.sum(hb_ref[...], axis=0)
     at = lax.broadcasted_iota(jnp.int32, rows.shape, 1)
     per = heads // wide
@@ -554,28 +523,23 @@
         for r in range(3):
             head_out[i : i + 1, r : r + 1] = picked[r : r + 1]
 
-    def total(out, got, recv, acc):
+    def total(out, got, which):
+        got[mine] = out[mine]
+        wait_for(got, slots - 1, in_sem.at[which])
+
         def add(k, acc):
-            slot = lax.rem(mine + (slots - k) * STRIDE_W, slots)
-            pltpu.make_async_copy(out.at[slot], got.at[slot], recv.at[slot]).wait()
-            return acc + got[slot].astype(F32)
-
-        return lax.fori_loop(1, slots, add, acc)
-
-    wbc_out[:, LANES:] = total(out_c, got_c, rwc_sem, out_c[mine].astype(F32))
-    wbc_out[:, :LANES] = total(out_b, got_b, rwb_sem, out_b[mine].astype(F32))
-    acc = total(out_d, got_d, rwd_sem, out_d[mine].astype(F32))
+            return acc + jnp.sum(got[pl.ds(k * group, group)].astype(F32), axis=0)
+
+        return lax.fori_loop(0, groups, add, jnp.zeros(got.shape[1:], F32))
+
+    wbc_out[:, LANES:] = total(out_c, got_c, 4)
+    wbc_out[:, :LANES] = total(out_b, got_b, 5)
+    acc = total(out_d, got_d, 6)
     wdt_out[0:16, :] = acc[:, :heads]
     wdt_out[16:32, :] = acc[:, heads : 2 * heads]
-
-    def done(k, _):
-        slot = lax.rem(mine + k, slots)
-        send_w(out_c, got_c, swc_sem, rwc_sem, slot).wait_send()
-        send_w(out_b, got_b, swb_sem, rwb_sem, slot).wait_send()
-        send_w(out_d, got_d, swd_sem, rwd_sem, slot).wait_send()
-        return 0
-
-    lax.fori_loop(1, slots, done, 0)
+    for which, ref in ((4, out_c), (5, out_b), (6, out_d)):
+        wait_for(ref, slots - 1, out_sem.at[which])
+    wait_for(hb_ref, groups - 1, out_sem.at[8])
 
 
 def place_kernel(
@@ -670,14 +634,14 @@
             v((slots, 32, LANES), BF),
             v((slots, 16, LANES), BF),
             dma((4, 4)),
-            dma((2, wide)),
+            dma((2,)),
             dma((5,)),
             dma((5,)),
-            dma((2, 8)),
-            dma((2, 8)),
-        ]
-        + [dma((wide,))] * 8
-        + [dma((slots,))] * 6,
+            dma((9,)),
+            dma((9,)),
+            dma((width // BLOCK,)),
+            dma((width // BLOCK,)),
+        ],
         compiler_params=pltpu.CompilerParams(
             collective_id=0, has_side_effects=True, vmem_limit_bytes=56 * 1024 * 1024
         ),

time: 98.5 us -> 86.1 us (0.87)
  Pallas kernels: 97.5 us -> 85.3 us
    pallas_call x1, Pallas kernels: 93.3 us -> 81.2 us  [local(): pl.pallas_call(functools.partial(scan_kernel, wide, dp), out_shape=(jax.S...]
where the time goes in v5:
time: 86.1 us; the launch traced here: 86 us
  Pallas kernels  85.3 us (99%)
    pallas_call x1, Pallas kernels, local(): pl.pallas_call(functools.partial(scan_kernel, wide, dp), out_shape=(jax.S...  81.2 us
    pallas_call x1, Pallas kernels, local(): pl.pallas_call(place_kernel, out_shape=tuple((jax.ShapeDtypeStruct(a.shap...  4.19 us

profile of v5, /device:TPU:1, one launch (start us, length us, event | category | flops | bytes accessed | tf_op | source)
XLA Modules:
  0.0 86.0 jit_solution(2916007189012943018)
XLA Ops:
  0.6 81.2 %scan_backward.1 = (bf16[256,4096]{1,0:T(8,128)(2,1)}, bf16[256,4096]{1,0:T(8,128)(2,1)}, f32[32,256]{1,0:T(8,128)}, f32[32,64]{1,0:T(8,128)}, f32[2,3]{1,0:T(2,128)}) custom-call(bf16[256,4096]{1,0:T(8,128)(2,1)} %bitcast.10, bf16[256,4096]{1,0:T(8,128)(2,1)} %bitcast.11, bf16[256,4096]{1,0:T(8,128)(2,1)} %bitcast.12, bf16[4096,256]{1,0:T(8,128)(2,1)} %wbc_hbm.1, ...), custom_call_target="tpu_custom_call" | custom-call | flops 8053063680 | bytes 8388608 | tf_op jit(solution)/shard_map/scan_backward/pallas_call | solution.py:582
  81.8 4.2 %place_results.1 = (bf16[256,4096]{1,0:T(8,128)(2,1)}, bf16[256,4096]{1,0:T(8,128)(2,1)}, f32[32,256]{1,0:T(8,128)}, f32[32,64]{1,0:T(8,128)}, f32[2,3]{1,0:T(2,128)}) custom-call(bf16[256,4096]{1,0:T(8,128)(2,1)} %get-tuple-element.15.x_in, bf16[256,4096]{1,0:T(8,128)(2,1)} %get-tuple-element.16.i_in, f32[32,256]{1,0:T(8,128)} %get-tuple-element.17.b_in, ...), custom_call_target="tpu_custom_call" | custom-call | tf_op jit(solution)/shard_map/place_results/pallas_call | solution.py:656

commit v6 on v5

--- a/solution.py
+++ b/solution.py
@@ -15,7 +15,7 @@
 STRIDE = 13
 STRIDE_W = 27
 WEIGHED = 16
-PIECES = 8
+PIECES = 2
 
 
 def mm(a, b):
@@ -39,9 +39,9 @@
 
 
 def scan_kernel(
-    wide, dp, in_hbm, x_hbm, g_hbm, wbc_hbm, wdt_hbm, alog_ref, bias_ref, skip_ref,
+    wide, dp, in_hbm, x_hbm, g_hbm, wbc_hbm, wdt_hbm, alog_hbm, bias_hbm, skip_hbm,
     xg_hbm, ig_hbm, wbc_out, wdt_out, head_out,
-    in_ref, x_ref, g_ref, wbc_ref, wdt_ref, f_ref, gt_ref, gotf_ref, gotg_ref, h_ref, p_ref,
+    small_ref, in_ref, x_ref, g_ref, wbc_ref, wdt_ref, end_ref, gote_ref, f_ref, gt_ref, gotf_ref, gotg_ref, h_ref, p_ref,
     goth_ref, gotp_ref, xs_ref, gs_ref, gxw_ref, int_ref, sib_ref, nt_ref, st_ref, lt_ref, rt_ref,
     col_ref, hrow_ref, xo_ref, io_ref, mine_c, mine_b, mine_d, sib_c, sib_b, sib_d,
     hg_ref, hsib_ref, ha_ref, hb_ref, out_c, out_b, out_d, got_c, got_b, got_d,
@@ -56,7 +56,7 @@
     slots = wide * sets
     mine = me * sets + place // 2
     seq, width = in_ref.shape
-    heads = alog_ref.shape[1]
+    heads = alog_hbm.shape[1]
     half = seq // 2
     nst = wbc_ref.shape[1] // 2
     owners = BLOCK // LANES
@@ -111,11 +111,17 @@
             pltpu.make_async_copy(wbc_hbm.at[part], wbc_ref.at[part], load_sem.at[1, q]),
             pltpu.make_async_copy(wdt_hbm.at[:, part], wdt_ref.at[:, part], load_sem.at[2, q]),
         ))
+    smalls = [
+        pltpu.make_async_copy(src, dst, load_sem.at[3, 2])
+        for src, dst in ((alog_hbm, small_ref.at[0]), (bias_hbm, small_ref.at[1]), (skip_hbm, small_ref.at[2]))
+    ]
     load_x = pltpu.make_async_copy(x_hbm, x_ref, load_sem.at[3, 0])
     load_g = pltpu.make_async_copy(g_hbm, g_ref, load_sem.at[3, 1])
     for load in loads:
         for one in load:
             one.start()
+    for one in smalls:
+        one.start()
     load_x.start()
     load_g.start()
 
@@ -141,6 +147,9 @@
     def send_f(peer):
         return remote(f_ref.at[peer], gotf_ref.at[me], out_sem.at[0], in_sem.at[0], {"wide": peer})
 
+    def send_e(peer):
+        return remote(end_ref.at[peer], gote_ref.at[me], out_sem.at[9], in_sem.at[9], {"wide": peer})
+
     def send_g(peer):
         return remote(gt_ref.at[peer], gotg_ref.at[me], out_sem.at[1], in_sem.at[1], {"wide": peer})
 
@@ -176,6 +185,7 @@
     sibling_d = remote(mine_d, sib_d, sib_send.at[3], sib_recv.at[3], sibling)
     sib_h = remote(hg_ref, hsib_ref, sib_send.at[4], sib_recv.at[4], sibling)
 
+    pltpu.make_async_copy(small_ref, small_ref, load_sem.at[3, 2]).wait()
     bc = jnp.zeros((seq, 2 * nst), F32)
     dt_raw = jnp.zeros((seq, heads), F32)
     for q, load in enumerate(loads):
@@ -190,9 +200,9 @@
     c_rows = bc[:, nst:]
     b_t = b_rows.astype(F32).T.astype(BF)
     c_t = c_rows.astype(F32).T.astype(BF)
-    dt_pre = dt_raw + bias_ref[...]
+    dt_pre = dt_raw + small_ref[1]
     dt = jnp.maximum(dt_pre, 0.0) + jnp.log1p(jnp.exp(-jnp.abs(dt_pre)))
-    rate = -jnp.exp(alog_ref[...])
+    rate = -jnp.exp(small_ref[0])
     log_rate = dt * rate
     pos_r = lax.broadcasted_iota(jnp.int32, (seq, seq), 0)
     pos_c = lax.broadcasted_iota(jnp.int32, (seq, seq), 1)
@@ -218,16 +228,18 @@
         r = spread(peers)
         xs = (columns(x_ref, peers).astype(F32) * mm(tail2, r)).astype(BF)
         f_t = mm(b_t, xs).astype(BF)
-        lq = mm(lq_rows, r).astype(BF)
+        ends = mm(lq_rows, r)
+        ends = ends[0:1] + ends[1:2] + ends[2:3]
         for i, peer in enumerate(peers):
             lanes = slice(i * LANES, (i + 1) * LANES)
             xs_ref[:, lanes_of(peer)] = xs[:, lanes]
-            f_ref[peer, :nst, :] = f_t[:, lanes]
-            f_ref[peer, nst:, :] = lq[:, lanes]
+            f_ref[peer] = f_t[:, lanes]
+            end_ref[peer] = ends[:, lanes]
 
             @pl.when(peer != me)
             def _():
                 send_f(peer).start()
+                send_e(peer).start()
 
         return 0
 
@@ -318,15 +330,16 @@
     lax.fori_loop(0, first_part, within, 0)
 
     def decay_of(i):
-        parts = gotf_ref[i, nst:, :].astype(F32)
-        return jnp.exp(parts[0:1] + parts[1:2] + parts[2:3])
+        return jnp.exp(gote_ref[i])
 
     gotf_ref[me] = f_ref[me]
+    gote_ref[me] = end_ref[me]
+    wait_for(gote_ref, wide - 1, in_sem.at[9])
     wait_for(gotf_ref, wide - 1, in_sem.at[0])
 
     def advance_f(i, state):
         h_ref[i] = state.astype(BF)
-        return state * decay_of(i) + gotf_ref[i, :nst, :].astype(F32)
+        return state * decay_of(i) + gotf_ref[i].astype(F32)
 
     start = jnp.zeros((nst, LANES), F32)
     lax.fori_loop(0, wide, advance_f, start)
@@ -362,7 +375,7 @@
     g_b = mm(n_low, c_rows)
     g_c = mm(nt_ref[...].T.astype(BF), b_rows)
 
-    skip_hi, skip_lo = split2(skip_ref[...])
+    skip_hi, skip_lo = split2(small_ref[2])
     skip_rows = jnp.concatenate(
         [jnp.concatenate([skip_hi, skip_lo], axis=1)]
         + [jnp.concatenate([v, none], axis=1) for v in (lq_hi, lq_mid, lq_lo)]
@@ -419,7 +432,6 @@
         for i, peer in enumerate(peers):
             cols = lanes_of(peer)
             xo_ref[:, cols] = gx[:, i * LANES : (i + 1) * LANES]
-            pltpu.make_async_copy(xo_ref.at[:, cols], xg_hbm.at[:, cols], store_sem.at[0]).start()
         return col_st, gb, sums
 
     def weigh(mine_p, sib_p, out, got, which, packed):
@@ -445,15 +457,19 @@
 
         lax.fori_loop(0, slots // WEIGHED, step_of, 0)
 
-    carried = lax.fori_loop(0, blocks // 4, finish_g, (zero_h, g_b, jnp.zeros((2, heads), F32)))
+    early_steps = blocks // 2
+    carried = lax.fori_loop(0, early_steps, finish_g, (zero_h, g_b, jnp.zeros((2, heads), F32)))
     sib_in.wait_recv()
     sibling_c.wait_recv()
     weigh(mine_c, sib_c, out_c, got_c, 4, False)
-    col_st, g_b, sums = lax.fori_loop(blocks // 4, blocks, finish_g, carried)
+    col_st, g_b, sums = lax.fori_loop(early_steps, blocks, finish_g, carried)
     mine_b[...] = g_b.astype(BF)
     sibling_b.start()
-
-    d_log = early - suffix(col_st) + sums[0:1]
+    store_x = pltpu.make_async_copy(xo_ref, xg_hbm, store_sem.at[0])
+    store_x.start()
+
+    late_hi, late_lo = split2(col_st)
+    d_log = early - mm(upper_all, late_hi) - mm(upper_all, late_lo) + sums[0:1]
     g_dt = (col_ref[...] + col_st) * ratio + rate * d_log * gate
     mine_d[...] = g_dt.astype(BF)
     sibling_d.start()
@@ -503,10 +519,10 @@
     lax.fori_loop(1, groups, start_b, 0)
     lax.fori_loop(blocks // 2, blocks, emit, 0)
 
-    for at, ref in enumerate((f_ref, gt_ref, h_ref, p_ref)):
+    for at, ref in ((0, f_ref), (1, gt_ref), (2, h_ref), (3, p_ref), (9, end_ref)):
         wait_for(ref, wide - 1, out_sem.at[at])
     wait_for(ha_ref, group - 1, out_sem.at[7])
-    pltpu.make_async_copy(xo_ref, xg_hbm, store_sem.at[0]).wait()
+    store_x.wait()
     pltpu.make_async_copy(io_ref, ig_hbm, store_sem.at[1]).wait()
     sib_in.wait_send()
     sibling_c.wait_send()
@@ -588,17 +604,20 @@
             jax.ShapeDtypeStruct((rows, heads), F32),
             jax.ShapeDtypeStruct((heads // wide, 3), F32),
         ),
-        in_specs=[any_spec] * 5 + [vmem] * 3,
+        in_specs=[any_spec] * 8,
         out_specs=(any_spec, any_spec, vmem, vmem, vmem),
         scratch_shapes=[
+            v((3, 1, heads), F32),
             v((seq, width), BF),
             v((seq, width), BF),
             v((seq, width), BF),
             v((width, 2 * nst), BF),
             v((heads, width), BF),
-            v((wide, nst + 16, LANES), BF),
+            v((wide, 1, LANES), F32),
+            v((wide, 1, LANES), F32),
             v((wide, nst, LANES), BF),
-            v((wide, nst + 16, LANES), BF),
+            v((wide, nst, LANES), BF),
+            v((wide, nst, LANES), BF),
             v((wide, nst, LANES), BF),
             v((wide, nst, LANES), BF),
             v((wide, nst, LANES), BF),
@@ -637,8 +656,8 @@
             dma((2,)),
             dma((5,)),
             dma((5,)),
-            dma((9,)),
-            dma((9,)),
+            dma((10,)),
+            dma((10,)),
             dma((width // BLOCK,)),
             dma((width // BLOCK,)),
         ],

time: 86.1 us -> 84.6 us (0.983)
  Pallas kernels: 85.3 us -> 83.9 us
    pallas_call x1, Pallas kernels: 81.2 us -> 80.1 us  [local(): pl.pallas_call(functools.partial(scan_kernel, wide, dp), out_shape=(jax.S...]
where the time goes in v6:
time: 84.6 us; the launch traced here: 84.5 us
  Pallas kernels  83.9 us (99%)
    pallas_call x1, Pallas kernels, local(): pl.pallas_call(functools.partial(scan_kernel, wide, dp), out_shape=(jax.S...  80.1 us
    pallas_call x1, Pallas kernels, local(): pl.pallas_call(place_kernel, out_shape=tuple((jax.ShapeDtypeStruct(a.shap...  3.77 us

profile of v6, /device:TPU:1, one launch (start us, length us, event | category | flops | bytes accessed | tf_op | source)
XLA Modules:
  0.0 84.5 jit_solution(16853244820355658423)
XLA Ops:
  0.6 80.1 %scan_backward.1 = (bf16[256,4096]{1,0:T(8,128)(2,1)}, bf16[256,4096]{1,0:T(8,128)(2,1)}, f32[32,256]{1,0:T(8,128)}, f32[32,64]{1,0:T(8,128)}, f32[2,3]{1,0:T(2,128)}) custom-call(bf16[256,4096]{1,0:T(8,128)(2,1)} %bitcast.10, bf16[256,4096]{1,0:T(8,128)(2,1)} %bitcast.11, bf16[256,4096]{1,0:T(8,128)(2,1)} %bitcast.12, bf16[4096,256]{1,0:T(8,128)(2,1)} %wbc_hbm.1, ...), custom_call_target="tpu_custom_call" | custom-call | flops 8053063680 | bytes 8388608 | tf_op jit(solution)/shard_map/scan_backward/pallas_call | solution.py:598
  80.8 3.8 %place_results.1 = (bf16[256,4096]{1,0:T(8,128)(2,1)}, bf16[256,4096]{1,0:T(8,128)(2,1)}, f32[32,256]{1,0:T(8,128)}, f32[32,64]{1,0:T(8,128)}, f32[2,3]{1,0:T(2,128)}) custom-call(bf16[256,4096]{1,0:T(8,128)(2,1)} %get-tuple-element.15.x_in, bf16[256,4096]{1,0:T(8,128)(2,1)} %get-tuple-element.16.i_in, f32[32,256]{1,0:T(8,128)} %get-tuple-element.17.b_in, ...), custom_call_target="tpu_custom_call" | custom-call | tf_op jit(solution)/shard_map/place_results/pallas_call | solution.py:675

commit v7 on v6

--- a/solution.py
+++ b/solution.py
@@ -481,30 +481,6 @@
     hg_ref[2:3, :heads] = sums[1:2]
     sib_h.start()
 
-    ga, gi = mine // group, lax.rem(mine, group)
-
-    def send_a(i):
-        return remote(ha_ref.at[gi], ha_ref.at[gi], out_sem.at[7], in_sem.at[7], at_slot(ga * group + i))
-
-    def send_b(i):
-        return remote(hb_ref.at[ga], hb_ref.at[ga], out_sem.at[8], in_sem.at[8], at_slot(i * group + gi))
-
-    def start_a(k, _):
-        send_a(lax.rem(gi + k, group)).start()
-        return 0
-
-    def start_b(k, _):
-        send_b(lax.rem(ga + k, groups)).start()
-        return 0
-
-    sibling_b.wait_recv()
-    weigh(mine_b, sib_b, out_b, got_b, 5, False)
-    sib_h.wait_recv()
-    ha_ref[gi] = hg_ref[...] + hsib_ref[...]
-    lax.fori_loop(1, group, start_a, 0)
-    sibling_d.wait_recv()
-    weigh(mine_d, sib_d, out_d, got_d, 6, True)
-
     def emit(j, _):
         cols = pl.ds(pl.multiple_of(j * BLOCK, BLOCK), BLOCK)
         d_in = mm_nt(mine_b[...], wbc_ref[cols, :nst]) + mm_nt(mine_c[...], wbc_ref[cols, nst:])
@@ -513,7 +489,32 @@
         pltpu.make_async_copy(io_ref.at[:, cols], ig_hbm.at[:, cols], store_sem.at[1]).start()
         return 0
 
-    lax.fori_loop(0, blocks // 2, emit, 0)
+    ga, gi = mine // group, lax.rem(mine, group)
+
+    def send_a(i):
+        return remote(ha_ref.at[gi], ha_ref.at[gi], out_sem.at[7], in_sem.at[7], at_slot(ga * group + i))
+
+    def send_b(i):
+        return remote(hb_ref.at[ga], hb_ref.at[ga], out_sem.at[8], in_sem.at[8], at_slot(i * group + gi))
+
+    def start_a(k, _):
+        send_a(lax.rem(gi + k, group)).start()
+        return 0
+
+    def start_b(k, _):
+        send_b(lax.rem(ga + k, groups)).start()
+        return 0
+
+    sibling_b.wait_recv()
+    weigh(mine_b, sib_b, out_b, got_b, 5, False)
+    sib_h.wait_recv()
+    ha_ref[gi] = hg_ref[...] + hsib_ref[...]
+    lax.fori_loop(1, group, start_a, 0)
+    lax.fori_loop(0, 2, emit, 0)
+    sibling_d.wait_recv()
+    weigh(mine_d, sib_d, out_d, got_d, 6, True)
+
+    lax.fori_loop(2, blocks // 2, emit, 0)
     wait_for(ha_ref, group - 1, in_sem.at[7])
     hb_ref[ga] = jnp.sum(ha_ref[...], axis=0)
     lax.fori_loop(1, groups, start_b, 0)

time: 84.6 us -> 84.6 us (level)
  no operation moved by 1% of the time
where the time goes in v7:
time: 84.6 us; the launch traced here: 84.5 us
  Pallas kernels  83.9 us (99%)
    pallas_call x1, Pallas kernels, local(): pl.pallas_call(functools.partial(scan_kernel, wide, dp), out_shape=(jax.S...  80.1 us
    pallas_call x1, Pallas kernels, local(): pl.pallas_call(place_kernel, out_shape=tuple((jax.ShapeDtypeStruct(a.shap...  3.77 us

profile of v7, /device:TPU:1, one launch (start us, length us, event | category | flops | bytes accessed | tf_op | source)
XLA Modules:
  0.0 84.5 jit_solution(1361111479063112184)
XLA Ops:
  0.6 80.1 %scan_backward.1 = (bf16[256,4096]{1,0:T(8,128)(2,1)}, bf16[256,4096]{1,0:T(8,128)(2,1)}, f32[32,256]{1,0:T(8,128)}, f32[32,64]{1,0:T(8,128)}, f32[2,3]{1,0:T(2,128)}) custom-call(bf16[256,4096]{1,0:T(8,128)(2,1)} %bitcast.10, bf16[256,4096]{1,0:T(8,128)(2,1)} %bitcast.11, bf16[256,4096]{1,0:T(8,128)(2,1)} %bitcast.12, bf16[4096,256]{1,0:T(8,128)(2,1)} %wbc_hbm.1, ...), custom_call_target="tpu_custom_call" | custom-call | flops 8053063680 | bytes 8388608 | tf_op jit(solution)/shard_map/scan_backward/pallas_call | solution.py:599
  80.8 3.8 %place_results.1 = (bf16[256,4096]{1,0:T(8,128)(2,1)}, bf16[256,4096]{1,0:T(8,128)(2,1)}, f32[32,256]{1,0:T(8,128)}, f32[32,64]{1,0:T(8,128)}, f32[2,3]{1,0:T(2,128)}) custom-call(bf16[256,4096]{1,0:T(8,128)(2,1)} %get-tuple-element.15.x_in, bf16[256,4096]{1,0:T(8,128)(2,1)} %get-tuple-element.16.i_in, f32[32,256]{1,0:T(8,128)} %get-tuple-element.17.b_in, ...), custom_call_target="tpu_custom_call" | custom-call | tf_op jit(solution)/shard_map/place_results/pallas_call | solution.py:676

commit v8 on v7

--- a/solution.py
+++ b/solution.py
@@ -531,6 +531,16 @@
     sibling_d.wait_send()
     sib_h.wait_send()
 
+    def total(out, got, which):
+        got[mine] = out[mine]
+        wait_for(got, slots - 1, in_sem.at[which])
+
+        def add(k, acc):
+            return acc + jnp.sum(got[pl.ds(k * group, group)].astype(F32), axis=0)
+
+        return lax.fori_loop(0, groups, add, jnp.zeros(got.shape[1:], F32))
+
+    wbc_out[:, LANES:] = total(out_c, got_c, 4)
     wait_for(hb_ref, groups - 1, in_sem.at[8])
     rows = jnp.sum(hb_ref[...], axis=0)
     at = lax.broadcasted_iota(jnp.int32, rows.shape, 1)
@@ -540,16 +550,6 @@
         for r in range(3):
             head_out[i : i + 1, r : r + 1] = picked[r : r + 1]
 
-    def total(out, got, which):
-        got[mine] = out[mine]
-        wait_for(got, slots - 1, in_sem.at[which])
-
-        def add(k, acc):
-            return acc + jnp.sum(got[pl.ds(k * group, group)].astype(F32), axis=0)
-
-        return lax.fori_loop(0, groups, add, jnp.zeros(got.shape[1:], F32))
-
-    wbc_out[:, LANES:] = total(out_c, got_c, 4)
     wbc_out[:, :LANES] = total(out_b, got_b, 5)
     acc = total(out_d, got_d, 6)
     wdt_out[0:16, :] = acc[:, :heads]

time: 84.6 us -> 84.5 us (level)
  no operation moved by 1% of the time
where the time goes in v8:
time: 84.5 us; the launch traced here: 84.4 us
  Pallas kernels  83.8 us (99%)
    pallas_call x1, Pallas kernels, local(): pl.pallas_call(functools.partial(scan_kernel, wide, dp), out_shape=(jax.S...  80 us
    pallas_call x1, Pallas kernels, local(): pl.pallas_call(place_kernel, out_shape=tuple((jax.ShapeDtypeStruct(a.shap...  3.77 us

profile of v8, /device:TPU:1, one launch (start us, length us, event | category | flops | bytes accessed | tf_op | source)
XLA Modules:
  0.0 84.4 jit_solution(9024959072324465674)
XLA Ops:
  0.6 80.0 %scan_backward.1 = (bf16[256,4096]{1,0:T(8,128)(2,1)}, bf16[256,4096]{1,0:T(8,128)(2,1)}, f32[32,256]{1,0:T(8,128)}, f32[32,64]{1,0:T(8,128)}, f32[2,3]{1,0:T(2,128)}) custom-call(bf16[256,4096]{1,0:T(8,128)(2,1)} %bitcast.10, bf16[256,4096]{1,0:T(8,128)(2,1)} %bitcast.11, bf16[256,4096]{1,0:T(8,128)(2,1)} %bitcast.12, bf16[4096,256]{1,0:T(8,128)(2,1)} %wbc_hbm.1, ...), custom_call_target="tpu_custom_call" | custom-call | flops 8053063680 | bytes 8388608 | tf_op jit(solution)/shard_map/scan_backward/pallas_call | solution.py:599
  80.6 3.8 %place_results.1 = (bf16[256,4096]{1,0:T(8,128)(2,1)}, bf16[256,4096]{1,0:T(8,128)(2,1)}, f32[32,256]{1,0:T(8,128)}, f32[32,64]{1,0:T(8,128)}, f32[2,3]{1,0:T(2,128)}) custom-call(bf16[256,4096]{1,0:T(8,128)(2,1)} %get-tuple-element.15.x_in, bf16[256,4096]{1,0:T(8,128)(2,1)} %get-tuple-element.16.i_in, f32[32,256]{1,0:T(8,128)} %get-tuple-element.17.b_in, ...), custom_call_target="tpu_custom_call" | custom-call | tf_op jit(solution)/shard_map/place_results/pallas_call | solution.py:676
